TPU v7x, 32 devices: a whole 2x2x4 slice. The times are simulated.
32 devices in a mesh: groups: 2 (over x), tile: 16 (over z, y, core).
Axes of the slice: x: 2, y: 2, z: 4, core: 2. Of those that a mesh axis runs over, the one named last changes fastest.
Arguments:
- gauss_params: float32 [14, 524288], P(None, ('groups', 'tile')), parts along dimension 1
- wanted: int32 [32, 16, 1024], P(('groups', 'tile')), parts along dimension 0, may hold values from 0 to 16383, as said below
- depth_order: int32 [512, 1024], P(('groups', 'tile')), parts along dimension 0, may hold values from 0 to 16383, as said below
- block_count: int32 [512], P(('groups', 'tile')), parts along dimension 0, may hold values from 1 to 8, as said below
- image_grad: float32 [512, 3, 256], P(('groups', 'tile')), parts along dimension 0, may hold values from -6 to 6
Outputs:
- image: float32 [512, 3, 256], P(('groups', 'tile')), parts along dimension 0
- param_grads: float32 [14, 524288], P(None, ('groups', 'tile')), parts along dimension 1
There are 2 independent parts, one for each index of `groups`. A program takes and returns all parts, laid end to end along the dimension named above; each array names one. Nothing has to cross between parts.
Inputs may be any that keep to these rules, and one draw needn't show every extreme that they name: `wanted`: for each source device, every one of its 16384 local rows is requested by exactly one device at exactly one position. `depth_order`: the lists of one device's 16 tiles together name every position of its received list exactly once. `block_count`: every device owns a tile with 8 blocks; entries of depth_order beyond a tile's block count are not read.
All inputs are finite; a program needn't handle non-finite values.
Results may differ from a plain program's by a relative error of at most 0.0003.
Values sent between devices are 32-bit elements; how exact they have to be, the bound alone decides.
No kernel may reach another device: no remote copies, remote signals or barrier semaphores. Data moves between devices by JAX's collectives and lax.ppermute only.
A program may use at most 192 MiB of HBM per device.

v0:
```python
import jax
import jax.numpy as jnp
from jax import lax
from jax.sharding import PartitionSpec as P

BLOCK = 128
PIX = 256


focal = 1000.0
center_u = 512.0
center_v = 512.0
dilate = 0.3
tile_row = 64
group_width = 4


def project(raw):
    pos_x, pos_y, depth = (raw[0], raw[1], raw[2])
    scale_x, scale_y, scale_z = (jnp.exp(raw[3]), jnp.exp(raw[4]), jnp.exp(raw[5]))
    norm_inv = 1.0 / jnp.sqrt(raw[6] * raw[6] + raw[7] * raw[7] + raw[8] * raw[8] + raw[9] * raw[9])
    q_real, q_one, q_two, q_three = (
        raw[6] * norm_inv,
        raw[7] * norm_inv,
        raw[8] * norm_inv,
        raw[9] * norm_inv,
    )
    rot = [
        [
            1.0 - 2.0 * (q_two * q_two + q_three * q_three),
            2.0 * (q_one * q_two - q_real * q_three),
            2.0 * (q_one * q_three + q_real * q_two),
        ],
        [
            2.0 * (q_one * q_two + q_real * q_three),
            1.0 - 2.0 * (q_one * q_one + q_three * q_three),
            2.0 * (q_two * q_three - q_real * q_one),
        ],
        [
            2.0 * (q_one * q_three - q_real * q_two),
            2.0 * (q_two * q_three + q_real * q_one),
            1.0 - 2.0 * (q_one * q_one + q_two * q_two),
        ],
    ]
    scales = [scale_x, scale_y, scale_z]
    mixed = [[rot[i][k] * scales[k] for k in range(3)] for i in range(3)]
    cov = [
        [
            mixed[i][0] * mixed[j][0] + mixed[i][1] * mixed[j][1] + mixed[i][2] * mixed[j][2]
            for j in range(3)
        ]
        for i in range(3)
    ]
    jac_uu = focal / depth
    jac_uz = -focal * pos_x / (depth * depth)
    jac_vv = focal / depth
    jac_vz = -focal * pos_y / (depth * depth)
    upper = [jac_uu * cov[0][k] + jac_uz * cov[2][k] for k in range(3)]
    lower = [jac_vv * cov[1][k] + jac_vz * cov[2][k] for k in range(3)]
    first = upper[0] * jac_uu + upper[2] * jac_uz + dilate
    cross = upper[1] * jac_vv + upper[2] * jac_vz
    second = lower[1] * jac_vv + lower[2] * jac_vz + dilate
    det_inv = 1.0 / (first * second - cross * cross)
    return jnp.stack(
        [
            focal * pos_x / depth + center_u,
            focal * pos_y / depth + center_v,
            second * det_inv,
            -cross * det_inv,
            first * det_inv,
            jax.nn.sigmoid(raw[10]),
            raw[11],
            raw[12],
            raw[13],
        ]
    )


def pixels(tile_ids):
    pixel = jnp.arange(256, dtype=jnp.int32)
    pixel_u = (16 * (tile_ids % tile_row))[:, None] + (pixel % 16)[None, :]
    pixel_v = (16 * (tile_ids // tile_row))[:, None] + (pixel // 16)[None, :]
    return (pixel_u.astype(jnp.float32) + 0.5, pixel_v.astype(jnp.float32) + 0.5)


def earlier_table(count):
    index = jnp.arange(count, dtype=jnp.int32)
    return (index[:, None] < index[None, :]).astype(jnp.float32)


def blend(trans, rows, pixel_u, pixel_v, alive):
    delta_u = pixel_u[:, :, None] - rows[0][:, None, :]
    delta_v = pixel_v[:, :, None] - rows[1][:, None, :]
    power = (
        -0.5 * (rows[2][:, None, :] * delta_u * delta_u + rows[4][:, None, :] * delta_v * delta_v)
        - rows[3][:, None, :] * delta_u * delta_v
    )
    alpha = rows[5][:, None, :] * jnp.exp(power) * alive[:, None, None]
    logs = jnp.log1p(-alpha)
    table = earlier_table(alpha.shape[2])
    before = jnp.exp(jnp.einsum("mpi,ik->mpk", logs, table, precision=lax.Precision.HIGHEST))
    weight = trans[:, :, None] * before * alpha
    contrib = jnp.einsum("mpk,cmk->mcp", weight, rows[6:9], precision=lax.Precision.HIGHEST)
    last_keep = before[:, :, -1] * (1.0 - alpha[:, :, -1])
    return (contrib, trans * last_keep)


def render_group(
    picture, buffer_grad, members, rounds, buffer, depth_order, block_count, image_grad, first_tile
):
    width = members.shape[0]
    block_total = depth_order.shape[1] // BLOCK
    orders = jnp.take(depth_order, members, axis=0)
    counts = jnp.take(block_count, members)
    pixel_u, pixel_v = pixels(first_tile + members)
    upstream = jnp.take(image_grad, members, axis=0)

    def block_rows(index):
        slots = lax.dynamic_slice_in_dim(orders, index * BLOCK, BLOCK, 1)
        return (slots, jnp.take(buffer, slots, axis=1))

    def forward(index, carry):
        trans, image, saved = carry
        slots, rows = block_rows(index)
        alive = (index < counts).astype(jnp.float32)
        contrib, trans_out = blend(trans, rows, pixel_u, pixel_v, alive)
        saved = lax.dynamic_update_index_in_dim(saved, trans, index, 0)
        return (trans_out, image + contrib, saved)

    start = (
        jnp.ones((width, PIX), jnp.float32),
        jnp.zeros((width, 3, PIX), jnp.float32),
        jnp.zeros((block_total, width, PIX), jnp.float32),
    )
    _, image, saved = lax.fori_loop(0, rounds, forward, start)

    def backward(step, carry):
        trans_grad, grads = carry
        index = rounds - 1 - step
        slots, rows = block_rows(index)
        alive = (index < counts).astype(jnp.float32)
        trans = lax.dynamic_index_in_dim(saved, index, 0, keepdims=False)
        _, pull = jax.vjp(
            lambda state, block: blend(state, block, pixel_u, pixel_v, alive), trans, rows
        )
        trans_in_grad, rows_grad = pull((upstream, trans_grad))
        grads = grads.at[:, slots].add(rows_grad)
        return (trans_in_grad, grads)

    _, buffer_grad = lax.fori_loop(
        0, rounds, backward, (jnp.zeros((width, PIX), jnp.float32), buffer_grad)
    )
    picture = picture.at[members].set(image)
    return (picture, buffer_grad)


def local(gauss_params, wanted, depth_order, block_count, image_grad):
    peer_count = lax.axis_size("tile")
    my_index = lax.axis_index("tile")
    tiles_here, slot_total = depth_order.shape
    capacity = wanted.shape[2]
    gauss_here = gauss_params.shape[1]
    asked = lax.all_to_all(wanted[0], "tile", split_axis=0, concat_axis=0, tiled=True)
    flat_asked = asked.reshape(-1)
    projected, project_pull = jax.vjp(project, gauss_params)
    outgoing = jnp.take(projected, flat_asked, axis=1).reshape(9, peer_count, capacity)
    arrived = lax.all_to_all(outgoing, "tile", split_axis=1, concat_axis=1, tiled=True)
    buffer = arrived.reshape(9, peer_count * capacity)
    first_tile = my_index * tiles_here
    width = min(group_width, tiles_here)
    group_total = tiles_here // width
    block_total = slot_total // BLOCK

    def one_group(group, carry):
        members = group * width + jnp.arange(width, dtype=jnp.int32)
        return render_group(
            carry[0],
            carry[1],
            members,
            block_total,
            buffer,
            depth_order,
            block_count,
            image_grad,
            first_tile,
        )

    start = (jnp.zeros((tiles_here, 3, PIX), jnp.float32), jnp.zeros_like(buffer))
    picture, buffer_grad = lax.fori_loop(0, group_total, one_group, start)
    returned = lax.all_to_all(
        buffer_grad.reshape(9, peer_count, capacity),
        "tile",
        split_axis=1,
        concat_axis=1,
        tiled=True,
    )
    summed = (
        jnp.zeros((9, gauss_here), jnp.float32)
        .at[:, flat_asked]
        .add(returned.reshape(9, peer_count * capacity))
    )
    param_grads = project_pull(summed)[0]
    return (picture, param_grads)


def solution(mesh):
    placed = (
        P(None, ("groups", "tile")),
        P(("groups", "tile"), None, None),
        P(("groups", "tile"), None),
        P(("groups", "tile")),
        P(("groups", "tile"), None, None),
    )
    return jax.shard_map(
        local,
        mesh=mesh,
        in_specs=placed,
        out_specs=(P(("groups", "tile"), None, None), P(None, ("groups", "tile"))),
        check_vma=False,
    )
```

profile of v0, /device:TPU:0, one launch (start us, length us, event | category | flops | bytes accessed | tf_op | source)
XLA Modules:
  0.0 1329.4 jit_solution(17702843148351409969)
XLA Ops:
  54.0 35.1 %stack.3 = f32[9,16384]{0,1:T(8,128)} concatenate(f32[1,16384]{0,1:T(8,128)} %copy.292, f32[1,16384]{0,1:T(8,128)} %copy.293, f32[1,16384]{0,1:T(8,128)} %copy.294, f32[1,16384]{0,1:T(8,128)} %copy.295, f32[1,16384]{0,1:T(8,128)} %copy.296, f32[1,16384]{0,1:T(8,128)} %copy.297, f32[3,16384]{0,1:T(8,128)} %copy.298), dimensions={0} | concatenate | bytes 1179648 | tf_op jit(solution)/shard_map/jvp()/stack | solution.py:64
  89.3 57.9 %gather_fusion.5 = f32[16384,9]{1,0:T(8,128)} fusion(f32[9,16384]{0,1:T(8,128)} %stack.3, s32[16384]{0:T(1024)S(1)} %broadcast_clamp_fusion), kind=kCustom, calls=%fused_computation.5 | custom fusion | bytes 1245184 | tf_op jit(solution)/shard_map/jit(_take)/gather | solution.py:166
  159.7 22.8 %all-to-all-done.1 = f32[9,16,1024]{2,0,1:T(8,128)S(1)} async-done(((f32[9,16,1024]{2,0,1:T(8,128)}), f32[9,16,1024]{2,0,1:T(8,128)S(1)}, u32[]{:S(2)}, u32[]{:S(2)}) %all-to-all-start.1) | async-done | bytes 589856 | tf_op jit(solution)/shard_map/all_to_all | solution.py:167
  190.8 880.0 %while.99 = (s32[]{:T(128)}, f32[16,3,256]{2,1,0:T(4,128)S(1)}, f32[9,16384]{0,1:T(8,128)}, s32[16,1024]{1,0:T(8,128)S(1)}, s32[16]{0:T(128)S(1)}, /*index=5*/s3...) while((s32[]{:T(128)}, f32[16,3,256]{2,1,0:T(4,128)S(1)}, ...), condition=%wide.region_14.16_spmd, body=%wide.region_0.15_spmd.sunk | while | flops 638335680 | bytes 5726116 | solution.py:189
  192.8 57.2 %while.100 = (s32[]{:T(128)}, f32[4,256]{1,0:T(4,128)S(1)}, f32[4,3,256]{2,1,0:T(4,128)S(1)}, f32[8,4,256]{2,1,0:T(4,128)S(1)}, s32[4,1024]{1,0:T(4,128)S(1)}, /...) while((s32[]{:T(128)}, f32[4,256]{1,0:T(4,128)S(1)}, ...), condition=%wide.region_2.3_spmd.clone, body=%wide.region_1.2_spmd.clone.sunk | while | flops 211593232 | bytes 1873726 | solution.py:135
  250.7 160.1 %while.101 = (s32[]{:T(128)}, f32[4,256]{1,0:T(4,128)S(1)}, f32[9,16384]{0,1:T(8,128)}, s32[4,1024]{1,0:T(4,128)S(1)}, f32[9,16384]{0,1:T(8,128)}, /*index=5*/s3...) while((s32[]{:T(128)}, f32[4,256]{1,0:T(4,128)S(1)}, ...), condition=%wide.region_13.14_spmd.clone, body=%wide.region_4.13_spmd.clone.sunk | while | flops 426731008 | bytes 3693989 | solution.py:150
  281.1 9.6 scatter_fusion
  301.1 9.6 scatter_fusion
  321.2 9.6 scatter_fusion
  361.2 9.6 scatter_fusion
  401.2 9.6 scatter_fusion
  412.8 57.2 %while.100 = (s32[]{:T(128)}, f32[4,256]{1,0:T(4,128)S(1)}, f32[4,3,256]{2,1,0:T(4,128)S(1)}, f32[8,4,256]{2,1,0:T(4,128)S(1)}, s32[4,1024]{1,0:T(4,128)S(1)}, /...) while((s32[]{:T(128)}, f32[4,256]{1,0:T(4,128)S(1)}, ...), condition=%wide.region_2.3_spmd.clone, body=%wide.region_1.2_spmd.clone.sunk | while | flops 211593232 | bytes 1873726 | solution.py:135
  470.7 160.1 %while.101 = (s32[]{:T(128)}, f32[4,256]{1,0:T(4,128)S(1)}, f32[9,16384]{0,1:T(8,128)}, s32[4,1024]{1,0:T(4,128)S(1)}, f32[9,16384]{0,1:T(8,128)}, /*index=5*/s3...) while((s32[]{:T(128)}, f32[4,256]{1,0:T(4,128)S(1)}, ...), condition=%wide.region_13.14_spmd.clone, body=%wide.region_4.13_spmd.clone.sunk | while | flops 426731008 | bytes 3693989 | solution.py:150
  481.1 9.6 scatter_fusion
  521.1 9.6 scatter_fusion
  561.2 9.6 scatter_fusion
  581.2 9.6 scatter_fusion
  632.8 57.2 %while.100 = (s32[]{:T(128)}, f32[4,256]{1,0:T(4,128)S(1)}, f32[4,3,256]{2,1,0:T(4,128)S(1)}, f32[8,4,256]{2,1,0:T(4,128)S(1)}, s32[4,1024]{1,0:T(4,128)S(1)}, /...) while((s32[]{:T(128)}, f32[4,256]{1,0:T(4,128)S(1)}, ...), condition=%wide.region_2.3_spmd.clone, body=%wide.region_1.2_spmd.clone.sunk | while | flops 211593232 | bytes 1873726 | solution.py:135
  690.7 160.1 %while.101 = (s32[]{:T(128)}, f32[4,256]{1,0:T(4,128)S(1)}, f32[9,16384]{0,1:T(8,128)}, s32[4,1024]{1,0:T(4,128)S(1)}, f32[9,16384]{0,1:T(8,128)}, /*index=5*/s3...) while((s32[]{:T(128)}, f32[4,256]{1,0:T(4,128)S(1)}, ...), condition=%wide.region_13.14_spmd.clone, body=%wide.region_4.13_spmd.clone.sunk | while | flops 426731008 | bytes 3693989 | solution.py:150
  852.8 57.2 %while.100 = (s32[]{:T(128)}, f32[4,256]{1,0:T(4,128)S(1)}, f32[4,3,256]{2,1,0:T(4,128)S(1)}, f32[8,4,256]{2,1,0:T(4,128)S(1)}, s32[4,1024]{1,0:T(4,128)S(1)}, /...) while((s32[]{:T(128)}, f32[4,256]{1,0:T(4,128)S(1)}, ...), condition=%wide.region_2.3_spmd.clone, body=%wide.region_1.2_spmd.clone.sunk | while | flops 211593232 | bytes 1873726 | solution.py:135
  910.7 160.1 %while.101 = (s32[]{:T(128)}, f32[4,256]{1,0:T(4,128)S(1)}, f32[9,16384]{0,1:T(8,128)}, s32[4,1024]{1,0:T(4,128)S(1)}, f32[9,16384]{0,1:T(8,128)}, /*index=5*/s3...) while((s32[]{:T(128)}, f32[4,256]{1,0:T(4,128)S(1)}, ...), condition=%wide.region_13.14_spmd.clone, body=%wide.region_4.13_spmd.clone.sunk | while | flops 426731008 | bytes 3693989 | solution.py:150
  1084.4 22.3 %all-to-all-done.2 = f32[9,16,1024]{2,0,1:T(8,128)S(1)} async-done(((f32[9,16,1024]{2,0,1:T(8,128)}), f32[9,16,1024]{2,0,1:T(8,128)S(1)}, u32[]{:S(2)}, u32[]{:S(2)}) %all-to-all-start.2) | async-done | bytes 589856 | tf_op jit(solution)/shard_map/all_to_all | solution.py:190
  1112.4 91.5 %scatter_custom_fusion.2 = f32[9,16384]{0,1:T(8,128)} fusion(s32[16384]{0:T(1024)} %bitcast.228, f32[16384,9]{1,0:T(8,128)} %copy.306, f32[]{:T(128)} %constant.415.clone.1), kind=kCustom, calls=%fused_computation.141 | custom fusion | flops 147456 | bytes 590336 | tf_op jit(solution)/shard_map/scatter-add | solution.py:200
  1203.9 59.2 %fusion.146 = (f32[1,16384]{0,1:T(8,128)}, f32[1,16384]{0,1:T(8,128)}, f32[1,16384]{0,1:T(8,128)}, f32[1,16384]{0,1:T(8,128)}, f32[1,16384]{0,1:T(8,128)}, /*ind...) fusion(f32[9,16384]{0,1:T(8,128)} %scatter_custom_fusion.2), kind=kLoop, calls=%fused_computation.336 | loop fusion | bytes 1179648 | tf_op jit(solution)/shard_map/transpose(jvp())/unstack | solution.py:64
  (1490 shorter events, 943.7 us)
Async XLA Ops:
  2.1 87.0 %all-to-all-start = ((s32[16,1,1024]{2,1,0:T(1,128)}), s32[16,1,1024]{2,1,0:T(1,128)S(1)}, u32[]{:S(2)}, u32[]{:S(2)}) async-start(s32[16,1,1024]{2,1,0:T(1,128)} %all_to_all.12), calls=%async_computation | async-start | bytes 131072 | tf_op jit(solution)/shard_map/all_to_all | solution.py:163
  18.0 31.2 %copy-start.13 = (f32[1,16384]{1,0:T(1,128)}, f32[1,16384]{1,0:T(1,128)S(1)}, u32[]{:S(2)}) copy-start(f32[1,16384]{1,0:T(1,128)S(1)} %get-tuple-element.1022) | copy-start | bytes 196612
  89.2 57.9 %copy-start.29 = (s32[16384,1]{0,1:T(1,128)}, s32[16384,1]{0,1:T(1,128)S(1)}, u32[]{:S(2)}) copy-start(s32[16384,1]{0,1:T(1,128)S(1)} %compare_select_fusion.7) | copy-start | bytes 196612
  147.1 12.5 copy-start.37
  153.5 29.0 %all-to-all-start.1 = ((f32[9,16,1024]{2,0,1:T(8,128)}), f32[9,16,1024]{2,0,1:T(8,128)S(1)}, u32[]{:S(2)}, u32[]{:S(2)}) async-start(f32[9,16,1024]{2,0,1:T(8,128)} %broadcast_select_fusion.4), calls=%async_computation.1 | async-start | bytes 2097152 | tf_op jit(solution)/shard_map/all_to_all | solution.py:167
  159.7 31.1 %copy-start = (s32[16]{0:T(128)S(1)}, s32[16]{0:T(128)}, u32[]{:S(2)}) copy-start(s32[16]{0:T(128)} %param.16) | copy-start | bytes 196
  159.7 31.1 %copy-start.1 = (s32[16,1024]{1,0:T(8,128)S(1)}, s32[16,1024]{1,0:T(8,128)}, u32[]{:S(2)}) copy-start(s32[16,1024]{1,0:T(8,128)} %param.15) | copy-start | bytes 196612
  1076.9 29.8 %all-to-all-start.2 = ((f32[9,16,1024]{2,0,1:T(8,128)}), f32[9,16,1024]{2,0,1:T(8,128)S(1)}, u32[]{:S(2)}, u32[]{:S(2)}) async-start(f32[9,16,1024]{2,0,1:T(8,128)} %copy.304), calls=%async_computation.2 | async-start | bytes 2097152 | tf_op jit(solution)/shard_map/all_to_all | solution.py:190
  1300.2 11.1 copy-start.2
  1300.2 11.1 copy-start.3
  1300.2 11.1 copy-start.4
  1300.2 11.1 copy-start.5
  1300.3 11.1 copy-start.6
  1300.3 11.1 copy-start.7
  1300.3 11.1 copy-start.8
  1300.3 11.1 copy-start.9
  1300.4 14.0 %copy-start.36 = (f32[1,16384]{1,0:T(1,128)S(1)}, f32[1,16384]{1,0:T(1,128)}, u32[]{:S(2)}) copy-start(f32[1,16384]{1,0:T(1,128)} %get-tuple-element.956) | copy-start | bytes 196612
  1305.9 19.1 %copy-start.14 = (f32[1,16384]{1,0:T(1,128)S(1)}, f32[1,16384]{1,0:T(1,128)}, u32[]{:S(2)}) copy-start(f32[1,16384]{1,0:T(1,128)} %copy-done.13) | copy-start | bytes 196612
  1305.9 19.1 %copy-start.34 = (f32[1,16384]{1,0:T(1,128)S(1)}, f32[1,16384]{1,0:T(1,128)}, u32[]{:S(2)}) copy-start(f32[1,16384]{1,0:T(1,128)} %get-tuple-element.969) | copy-start | bytes 196612
  1305.9 19.1 %copy-start.35 = (f32[1,16384]{1,0:T(1,128)S(1)}, f32[1,16384]{1,0:T(1,128)}, u32[]{:S(2)}) copy-start(f32[1,16384]{1,0:T(1,128)} %get-tuple-element.971) | copy-start | bytes 196612
  1305.9 19.7 %copy-start.30 = (f32[1,16384]{1,0:T(1,128)S(1)}, f32[1,16384]{1,0:T(1,128)}, u32[]{:S(2)}) copy-start(f32[1,16384]{1,0:T(1,128)} %get-tuple-element.961) | copy-start | bytes 196612
  1305.9 19.7 %copy-start.31 = (f32[1,16384]{1,0:T(1,128)S(1)}, f32[1,16384]{1,0:T(1,128)}, u32[]{:S(2)}) copy-start(f32[1,16384]{1,0:T(1,128)} %get-tuple-element.963) | copy-start | bytes 196612
  1305.9 19.7 %copy-start.32 = (f32[1,16384]{1,0:T(1,128)S(1)}, f32[1,16384]{1,0:T(1,128)}, u32[]{:S(2)}) copy-start(f32[1,16384]{1,0:T(1,128)} %get-tuple-element.974) | copy-start | bytes 196612
  1305.9 19.7 %copy-start.33 = (f32[1,16384]{1,0:T(1,128)S(1)}, f32[1,16384]{1,0:T(1,128)}, u32[]{:S(2)}) copy-start(f32[1,16384]{1,0:T(1,128)} %get-tuple-element.976) | copy-start | bytes 196612
  (17 other events, 157.7 us)
where the time goes:
time: 1340 us; the launch traced here: 1330 us
  local copies, waits for them, and re-layouts  569 us (42%)
  other arithmetic  470 us (35%)
  matrix products  216 us (16%)
  waiting for transfers between devices  45.1 us (3%)
  starting transfers between devices  20.4 us (2%)
    scatter-add x32, other arithmetic, backward(): grads = grads.at[:, slots].add(rows_grad)  308 us
    gather x128, local copies, waits for them, and re-layouts, block_rows(): return (slots, jnp.take(buffer, slots, axis=1))  289 us
    dot_general x96, matrix products, blend(): jnp.einsum('mpi,ik->mpk', logs, table, precision=lax.Precision.HIGHEST)  138 us
    another operation x2, local copies, waits for them, and re-layouts, project(): jnp.stack([focal * pos_x / depth + center_u, focal * pos_y / depth + cent...  94.4 us
    scatter-add x1, other arithmetic, local(): summed = jnp.zeros((9, gauss_here), jnp.float32).at[:, flat_asked].add(re...  91.5 us
    dot_general x96, matrix products, blend(): jnp.einsum('mpk,cmk->mcp', weight, rows[6:9], precision=lax.Precision.HIG...  77.7 us
    gather x2, local copies, waits for them, and re-layouts, local(): jnp.take(projected, flat_asked, axis=1).reshape(9, peer_count, capacity)  63.1 us
    unnamed x88, local copies, waits for them, and re-layouts  49.9 us
  transfers between devices with their start and end apart: 3, of which 2 were waited for; matrix products, arithmetic and copies ran while one was open for 6% of the time, Pallas kernels for 0%

commit v1 on v0

v1 whole, which is shorter than its diff:
```python
import jax
import jax.numpy as jnp
from jax import lax
from jax.experimental import pallas as pl
from jax.experimental.pallas import tpu as pltpu
from jax.sharding import PartitionSpec as P

BLOCK = 128
PIX = 256
LANES = 128
ROWS = 8
CHAN = 9
PARAMS = 14
FINE = 5

focal = 1000.0
center_u = 512.0
center_v = 512.0
dilate = 0.3
tile_row = 64
log_floor = -200.0
vmem_bytes = 56 * 1024 * 1024

f32 = jnp.float32
bf16 = jnp.bfloat16


def pieces(value, count):
    out = []
    for _ in range(count - 1):
        head = value.astype(bf16)
        out.append(head)
        value = value - head.astype(f32)
    out.append(value.astype(bf16))
    return out


def fill_table(read, table, table_low, fine):
    for c in range(CHAN):
        wide = jnp.concatenate([read(c, 0), read(c, 1)], axis=1)
        part = pieces(wide, 3 if c < fine else 2)
        rows = pl.ds(c * 64, 64)
        table[rows, 0:256] = part[0]
        table[rows, 256:512] = part[1]
        if c < fine:
            table_low[rows, :] = part[2]


def pick(index, table, table_low, fine):
    column = (index & 127) | ((index >> 13) << 7)
    row = (index >> 7) & 63
    places = lax.broadcasted_iota(jnp.int32, (256, 256), 0)
    chosen = (jnp.broadcast_to(column, (256, 256)) == places).astype(f32).astype(bf16)
    row_hit = jnp.broadcast_to(row, (64, 256)) == lax.broadcasted_iota(jnp.int32, (64, 256), 0)
    both = jnp.dot(
        table[...], jnp.concatenate([chosen, chosen], axis=0), preferred_element_type=f32
    )
    if fine:
        low = jnp.dot(table_low[...], chosen, preferred_element_type=f32)
    out = []
    for c in range(CHAN):
        mine = both[c * 64 : c * 64 + 64]
        if c < fine:
            mine = mine + low[c * 64 : c * 64 + 64]
        out.append(jnp.sum(jnp.where(row_hit, mine, 0.0), axis=0, keepdims=True))
    return out


def gather_all(index_ref, out_ref, table, table_low, fine):
    def step(t, carry):
        for half in range(ROWS // 2):
            index = jnp.concatenate(
                [index_ref[t, 2 * half : 2 * half + 1, :], index_ref[t, 2 * half + 1 : 2 * half + 2, :]],
                axis=1,
            )
            for c, line in enumerate(pick(index, table, table_low, fine)):
                out_ref[t, c, 2 * half : 2 * half + 1, :] = line[:, :LANES]
                out_ref[t, c, 2 * half + 1 : 2 * half + 2, :] = line[:, LANES:]
        return carry

    lax.fori_loop(0, index_ref.shape[0], step, 0)


def invert_kernel(index_ref, out_ref):
    place = lax.broadcasted_iota(jnp.int32, (LANES, LANES), 0)
    lane = lax.broadcasted_iota(jnp.int32, (LANES, LANES), 1).astype(f32)

    def step(t, total):
        for s in range(ROWS):
            line = index_ref[t, s : s + 1, :]
            row_hit = jnp.broadcast_to(line >> 7, (LANES, LANES)) == place
            column_hit = jnp.broadcast_to(line & 127, (LANES, LANES)) == place
            here = (t * ROWS + s).astype(f32)
            left = jnp.concatenate(
                [jnp.where(row_hit, here, 0.0).astype(bf16), jnp.where(row_hit, lane, 0.0).astype(bf16)],
                axis=0,
            )
            right = jnp.where(column_hit, 1.0, 0.0).astype(bf16)
            total = total + lax.dot_general(
                left, right, (((1,), (1,)), ((), ())), preferred_element_type=f32
            )
        return total

    total = lax.fori_loop(0, index_ref.shape[0], step, jnp.zeros((2 * LANES, LANES), f32))
    value = (total[:LANES] * float(LANES) + total[LANES:]).astype(jnp.int32)
    for t in range(index_ref.shape[0]):
        out_ref[t] = value[t * ROWS : t * ROWS + ROWS]


def project_core(raw):
    pos_x, pos_y, depth = (raw[0], raw[1], raw[2])
    scale_x, scale_y, scale_z = (jnp.exp(raw[3]), jnp.exp(raw[4]), jnp.exp(raw[5]))
    norm_inv = 1.0 / jnp.sqrt(raw[6] * raw[6] + raw[7] * raw[7] + raw[8] * raw[8] + raw[9] * raw[9])
    q_real, q_one, q_two, q_three = (
        raw[6] * norm_inv,
        raw[7] * norm_inv,
        raw[8] * norm_inv,
        raw[9] * norm_inv,
    )
    rot = [
        [
            1.0 - 2.0 * (q_two * q_two + q_three * q_three),
            2.0 * (q_one * q_two - q_real * q_three),
            2.0 * (q_one * q_three + q_real * q_two),
        ],
        [
            2.0 * (q_one * q_two + q_real * q_three),
            1.0 - 2.0 * (q_one * q_one + q_three * q_three),
            2.0 * (q_two * q_three - q_real * q_one),
        ],
        [
            2.0 * (q_one * q_three - q_real * q_two),
            2.0 * (q_two * q_three + q_real * q_one),
            1.0 - 2.0 * (q_one * q_one + q_two * q_two),
        ],
    ]
    scales = [scale_x, scale_y, scale_z]
    mixed = [[rot[i][k] * scales[k] for k in range(3)] for i in range(3)]
    cov = [
        [
            mixed[i][0] * mixed[j][0] + mixed[i][1] * mixed[j][1] + mixed[i][2] * mixed[j][2]
            for j in range(3)
        ]
        for i in range(3)
    ]
    depth_inv = 1.0 / depth
    jac_uu = focal * depth_inv
    jac_uz = -jac_uu * (pos_x * depth_inv)
    jac_vv = jac_uu
    jac_vz = -jac_uu * (pos_y * depth_inv)
    upper = [jac_uu * cov[0][k] + jac_uz * cov[2][k] for k in range(3)]
    lower = [jac_vv * cov[1][k] + jac_vz * cov[2][k] for k in range(3)]
    first = upper[0] * jac_uu + upper[2] * jac_uz + dilate
    cross = upper[1] * jac_vv + upper[2] * jac_vz
    second = lower[1] * jac_vv + lower[2] * jac_vz + dilate
    det_inv = 1.0 / (first * second - cross * cross)
    return [
        focal * pos_x * depth_inv + center_u,
        focal * pos_y * depth_inv + center_v,
        second * det_inv,
        -cross * det_inv,
        first * det_inv,
    ]


def sigmoid(x):
    return 1.0 / (1.0 + jnp.exp(-x))


def project_kernel(params_ref, out_ref, raw):
    def step(t, carry):
        for s in range(ROWS):
            raw[:, s, :] = params_ref[:, pl.ds(pl.multiple_of((t * ROWS + s) * LANES, LANES), LANES)]
        rows = project_core([raw[k] for k in range(10)])
        for c in range(5):
            out_ref[t, c] = rows[c]
        out_ref[t, 5] = sigmoid(raw[10])
        for c in range(3):
            out_ref[t, 6 + c] = raw[11 + c]
        return carry

    lax.fori_loop(0, out_ref.shape[0], step, 0)


def read_half(ref, c, half):
    groups = ref.shape[0] // 2
    return jnp.concatenate([ref[half * groups + q, c] for q in range(groups)], axis=0)


def gather_kernel(fine, index_ref, in_ref, out_ref, table, table_low):
    fill_table(lambda c, half: read_half(in_ref, c, half), table, table_low, fine)
    gather_all(index_ref, out_ref, table, table_low, fine)


def return_kernel(index_ref, grads_ref, params_ref, out_ref, table, table_low, summed, raw, stage):
    fill_table(lambda c, half: read_half(grads_ref, c, half), table, table_low, 0)
    gather_all(index_ref, summed, table, table_low, 0)

    def step(t, carry):
        for s in range(ROWS):
            raw[:, s, :] = params_ref[:, pl.ds(pl.multiple_of((t * ROWS + s) * LANES, LANES), LANES)]
        _, pull = jax.vjp(project_core, [raw[k] for k in range(10)])
        core = pull([summed[t, c] for c in range(5)])[0]
        for k in range(10):
            stage[k] = core[k]
        stage[10] = summed[t, 5] * sigmoid(-raw[10])
        for c in range(3):
            stage[11 + c] = summed[t, 6 + c]
        for s in range(ROWS):
            out_ref[:, pl.ds(pl.multiple_of((t * ROWS + s) * LANES, LANES), LANES)] = stage[:, s, :]
        return carry

    lax.fori_loop(0, grads_ref.shape[0], step, 0)


def scan_before(value, row):
    total = value
    for shift in (1, 2, 4):
        total = total * jnp.where(row >= shift, pltpu.roll(total, shift, 0), 1.0)
    before = jnp.where(row >= 1, pltpu.roll(total, 1, 0), 1.0)
    return before, total[ROWS - 1 : ROWS, :]


def scan_behind(gain, offset, row, incoming):
    for shift in (1, 2, 4):
        inside = row < ROWS - shift
        offset = offset + gain * jnp.where(inside, pltpu.roll(offset, ROWS - shift, 0), 0.0)
        gain = gain * jnp.where(inside, pltpu.roll(gain, ROWS - shift, 0), 1.0)
    value = offset + gain * incoming
    behind = jnp.where(row < ROWS - 1, pltpu.roll(value, ROWS - 1, 0), incoming)
    return behind, value[0:1, :]


def two_rows(value):
    head = value.astype(bf16)
    return head, (value - head.astype(f32)).astype(bf16)


def blend_kernel(
    count_ref,
    first_ref,
    slots_ref,
    upstream_ref,
    image_ref,
    grads_ref,
    features,
    basis,
    alpha_s,
    gc_s,
    weight_s,
    gain_s,
    offset_s,
    pair,
    moments,
    colour_grads,
):
    t = pl.program_id(0)
    tile = first_ref[0] + t
    count = count_ref[t]
    mid_u = ((tile % tile_row) * 16 + 8).astype(f32)
    mid_v = ((tile // tile_row) * 16 + 8).astype(f32)
    pixel = lax.broadcasted_iota(jnp.int32, (1, PIX), 1)
    x = (pixel & 15).astype(f32) - 7.5
    y = (pixel >> 4).astype(f32) - 7.5
    row = lax.broadcasted_iota(jnp.int32, (ROWS, PIX), 0)

    @pl.when(t == 0)
    def _():
        basis[...] = jnp.zeros_like(basis)
        features[...] = jnp.zeros_like(features)
        for k in range(3):
            for m, line in enumerate((jnp.ones_like(x), x, y, x * x, x * y, y * y)):
                basis[6 * k + m : 6 * k + m + 1, 0:PIX] = line

    monomials = jnp.concatenate(
        [jnp.ones_like(x), x, y, x * x, x * y, y * y, jnp.zeros((2, PIX), f32)], axis=0
    ).astype(bf16)
    up = upstream_ref[0]
    up_head = up.astype(bf16).astype(f32)
    up_tail = up - up_head
    basis[18:21, PIX:] = up_head
    basis[21:24, PIX:] = up_tail
    basis[24:27, PIX:] = up_head
    basis16 = basis[...].astype(bf16)
    up_both = jnp.concatenate([up_head, up_tail, jnp.zeros((2, PIX), f32)], axis=0).astype(bf16)

    off_u = mid_u - slots_ref[0, 0]
    off_v = mid_v - slots_ref[0, 1]
    con_a, con_b, con_c = (slots_ref[0, 2], slots_ref[0, 3], slots_ref[0, 4])
    log_op = jnp.maximum(jnp.log(slots_ref[0, 5]), log_floor)
    side_u = con_a * off_u + con_b * off_v
    side_v = con_b * off_u + con_c * off_v
    coefs = [
        log_op - 0.5 * (off_u * side_u + off_v * side_v),
        -side_u,
        -side_v,
        -0.5 * con_a,
        -con_b,
        -0.5 * con_c,
    ]
    for m, coef in enumerate(coefs):
        for k, part in enumerate(pieces(coef, 3)):
            features[:, 6 * k + m, :] = part.astype(f32)
    for c in range(3):
        head, tail = two_rows(slots_ref[0, 6 + c])
        features[:, 18 + c, :] = head.astype(f32)
        features[:, 21 + c, :] = head.astype(f32)
        features[:, 24 + c, :] = tail.astype(f32)
    image_ref[...] = jnp.zeros_like(image_ref)
    grads_ref[...] = jnp.zeros_like(grads_ref)
    moments[...] = jnp.zeros_like(moments)
    colour_grads[...] = jnp.zeros_like(colour_grads)

    def forward(b, carry):
        trans, image = carry
        block = features[b]
        both = lax.dot_general(
            block.astype(bf16), basis16, (((0,), (0,)), ((), ())), preferred_element_type=f32
        )
        prod = jnp.ones((ROWS, PIX), f32)
        ahead = jnp.zeros((ROWS, PIX), f32)
        local = []
        for i in range(BLOCK // ROWS):
            alpha = jnp.exp(both[i * ROWS : i * ROWS + ROWS, :PIX])
            gc = both[i * ROWS : i * ROWS + ROWS, PIX:]
            weight = prod * alpha
            ahead = ahead + weight * gc
            prod = prod - weight
            alpha_s[b, i] = alpha
            gc_s[b, i] = gc
            local.append(weight)
        gain_s[b] = prod
        offset_s[b] = ahead
        before, whole = scan_before(prod, row)
        before = before * trans
        heads, tails = [], []
        for i in range(BLOCK // ROWS):
            weight = local[i] * before
            weight_s[b, i] = weight
            head, tail = two_rows(weight)
            heads.append(head)
            tails.append(tail)
        w2 = jnp.concatenate(heads + tails, axis=0)
        head = block[18:21]
        tail = block[24:27]
        colour = jnp.concatenate(
            [
                jnp.concatenate([head, tail, jnp.zeros((2, BLOCK), f32)], axis=0),
                jnp.concatenate([head, jnp.zeros((5, BLOCK), f32)], axis=0),
            ],
            axis=1,
        ).astype(bf16)
        image = image + jnp.dot(colour, w2, preferred_element_type=f32)
        got = lax.dot_general(up_both, w2, (((1,), (1,)), ((), ())), preferred_element_type=f32)
        colour_grads[:, b, :] = got[0:3, :BLOCK] + got[0:3, BLOCK:] + got[3:6, :BLOCK]
        return (trans * whole, image)

    _, image = lax.fori_loop(
        0, count, forward, (jnp.ones((1, PIX), f32), jnp.zeros((ROWS, PIX), f32))
    )
    image_ref[0] = image[0:3] + image[3:6]

    def backward(step, incoming):
        b = count - 1 - step
        behind, start = scan_behind(gain_s[b], offset_s[b], row, incoming)
        heads, tails = [], []
        for i in reversed(range(BLOCK // ROWS)):
            diff = gc_s[b, i] - behind
            head, tail = two_rows(weight_s[b, i] * diff)
            heads.append(head)
            tails.append(tail)
            behind = behind + alpha_s[b, i] * diff
        h2 = jnp.concatenate(heads[::-1] + tails[::-1], axis=0)
        got = lax.dot_general(monomials, h2, (((1,), (1,)), ((), ())), preferred_element_type=f32)
        moments[:, b, :] = got[:, :BLOCK] + got[:, BLOCK:]
        return start

    lax.fori_loop(0, count, backward, jnp.zeros((1, PIX), f32))

    sum_h, sum_x, sum_y, sum_xx, sum_xy, sum_yy = [moments[m] for m in range(6)]
    sum_u = sum_x + off_u * sum_h
    sum_v = sum_y + off_v * sum_h
    grads_ref[0, 0] = con_a * sum_u + con_b * sum_v
    grads_ref[0, 1] = con_b * sum_u + con_c * sum_v
    grads_ref[0, 2] = -0.5 * (sum_xx + off_u * (sum_x + sum_u))
    grads_ref[0, 3] = -(sum_xy + off_v * sum_x + off_u * sum_v)
    grads_ref[0, 4] = -0.5 * (sum_yy + off_v * (sum_y + sum_v))
    grads_ref[0, 5] = sum_h
    for c in range(3):
        grads_ref[0, 6 + c] = colour_grads[c]


def params(**kw):
    return pltpu.CompilerParams(vmem_limit_bytes=vmem_bytes, **kw)


def local(gauss_params, wanted, depth_order, block_count, image_grad):
    peers = wanted.shape[1]
    capacity = wanted.shape[2]
    tiles_here, slots = depth_order.shape
    gauss_here = gauss_params.shape[1]
    lines = capacity // LANES
    groups = gauss_here // (ROWS * LANES)
    blocks = slots // BLOCK
    shape = (groups, CHAN, ROWS, LANES)
    index_shape = (groups, ROWS, LANES)
    tables = [
        pltpu.VMEM((CHAN * 64, 512), bf16),
        pltpu.VMEM((FINE * 64, 256), bf16),
    ]

    def exchange(value):
        if lines != ROWS:
            value = value.transpose(0, 2, 1, 3).reshape(peers, lines, CHAN, LANES).transpose(0, 2, 1, 3)
        value = lax.all_to_all(value, "tile", split_axis=0, concat_axis=0, tiled=True)
        if lines != ROWS:
            value = value.transpose(0, 2, 1, 3).reshape(groups, ROWS, CHAN, LANES).transpose(0, 2, 1, 3)
        return value

    def invert(index):
        return pl.pallas_call(
            invert_kernel,
            out_shape=jax.ShapeDtypeStruct(index_shape, jnp.int32),
            compiler_params=params(),
        )(index)

    def gather(index, value, fine):
        return pl.pallas_call(
            lambda *refs: gather_kernel(fine, *refs),
            out_shape=jax.ShapeDtypeStruct(shape, f32),
            scratch_shapes=tables,
            compiler_params=params(),
        )(index, value)

    asked = lax.all_to_all(
        wanted.reshape(peers, lines, LANES), "tile", split_axis=0, concat_axis=0, tiled=True
    ).reshape(index_shape)
    projected = pl.pallas_call(
        project_kernel,
        out_shape=jax.ShapeDtypeStruct(shape, f32),
        scratch_shapes=[pltpu.VMEM((PARAMS, ROWS, LANES), f32)],
        compiler_params=params(),
    )(gauss_params)
    order = (
        depth_order.reshape(tiles_here, blocks, ROWS, BLOCK // ROWS)
        .transpose(0, 1, 3, 2)
        .reshape(tiles_here, blocks, BLOCK)
    )
    order_back = invert(order)
    outgoing = gather(asked, projected, FINE)
    arrived = exchange(outgoing)
    asked_back = invert(asked)
    slots_in = gather(order, arrived, FINE)
    first_tile = (lax.axis_index("tile") * tiles_here).reshape(1).astype(jnp.int32)
    steps = BLOCK // ROWS
    image, slot_grads = pl.pallas_call(
        blend_kernel,
        grid=(tiles_here,),
        in_specs=[
            pl.BlockSpec(memory_space=pltpu.SMEM),
            pl.BlockSpec(memory_space=pltpu.SMEM),
            pl.BlockSpec((1, CHAN, blocks, BLOCK), lambda t: (t, 0, 0, 0)),
            pl.BlockSpec((1, 3, PIX), lambda t: (t, 0, 0)),
        ],
        out_specs=[
            pl.BlockSpec((1, 3, PIX), lambda t: (t, 0, 0)),
            pl.BlockSpec((1, CHAN, blocks, BLOCK), lambda t: (t, 0, 0, 0)),
        ],
        out_shape=[
            jax.ShapeDtypeStruct((tiles_here, 3, PIX), f32),
            jax.ShapeDtypeStruct((tiles_here, CHAN, blocks, BLOCK), f32),
        ],
        scratch_shapes=[
            pltpu.VMEM((blocks, 32, BLOCK), f32),
            pltpu.VMEM((32, 2 * PIX), f32),
            pltpu.VMEM((blocks, steps, ROWS, PIX), f32),
            pltpu.VMEM((blocks, steps, ROWS, PIX), f32),
            pltpu.VMEM((blocks, steps, ROWS, PIX), f32),
            pltpu.VMEM((blocks, ROWS, PIX), f32),
            pltpu.VMEM((blocks, ROWS, PIX), f32),
            pltpu.VMEM((8, 128), f32),
            pltpu.VMEM((8, blocks, BLOCK), f32),
            pltpu.VMEM((3, blocks, BLOCK), f32),
        ],
        compiler_params=params(),
    )(block_count, first_tile, slots_in, image_grad)
    returned = exchange(gather(order_back, slot_grads, 0))
    param_grads = pl.pallas_call(
        return_kernel,
        out_shape=jax.ShapeDtypeStruct(gauss_params.shape, f32),
        scratch_shapes=tables
        + [
            pltpu.VMEM(shape, f32),
            pltpu.VMEM((PARAMS, ROWS, LANES), f32),
            pltpu.VMEM((PARAMS, ROWS, LANES), f32),
        ],
        compiler_params=params(),
    )(asked_back, returned, gauss_params)
    return (image, param_grads)


def solution(mesh):
    placed = (
        P(None, ("groups", "tile")),
        P(("groups", "tile"), None, None),
        P(("groups", "tile"), None),
        P(("groups", "tile")),
        P(("groups", "tile"), None, None),
    )
    return jax.shard_map(
        local,
        mesh=mesh,
        in_specs=placed,
        out_specs=(P(("groups", "tile"), None, None), P(None, ("groups", "tile"))),
        check_vma=False,
    )
```

time: 1340 us -> 200 us (0.15)
  the two profiles are of different devices: /device:TPU:0 before, /device:TPU:11 now
where the time goes in v1:
time: 200 us; the launch traced here: 204 us
  Pallas kernels  122 us (61%)
  starting transfers between devices  57.6 us (29%)
  waiting for transfers between devices  16.7 us (8%)
  local copies, waits for them, and re-layouts  6.59 us (3%)
    all_to_all x2, starting transfers between devices, exchange(): lax.all_to_all(value, 'tile', split_axis=0, concat_axis=0, tiled=True)  51 us
    pallas_call x3, Pallas kernels, gather(): pl.pallas_call(lambda *refs: gather_kernel(fine, *refs), out_shape=jax.Sh...  50.4 us
    pallas_call x1, Pallas kernels, local(): pl.pallas_call(blend_kernel, grid=(tiles_here,), in_specs=[pl.BlockSpec(m...  37.2 us
    pallas_call x1, Pallas kernels, local(): pl.pallas_call(return_kernel, out_shape=jax.ShapeDtypeStruct(gauss_params...  18.3 us
    all_to_all x2, waiting for transfers between devices, exchange(): lax.all_to_all(value, 'tile', split_axis=0, concat_axis=0, tiled=True)  15.1 us
    pallas_call x2, Pallas kernels, invert(): pl.pallas_call(invert_kernel, out_shape=jax.ShapeDtypeStruct(index_shape,...  13.1 us
    all_to_all x1, starting transfers between devices, local(): lax.all_to_all(wanted.reshape(peers, lines, LANES), 'tile', split_axis=0,...  6.61 us
    unnamed x15, local copies, waits for them, and re-layouts  5.21 us
  transfers between devices with their start and end apart: 3, of which 3 were waited for; matrix products, arithmetic and copies ran while one was open for 1% of the time, Pallas kernels for 8%

profile of v1, /device:TPU:11, one launch (start us, length us, event | category | flops | bytes accessed | tf_op | source)
XLA Modules:
  0.0 204.1 jit_solution(11221180421372462489)
XLA Ops:
  0.6 1.5 copy.15
  2.1 6.6 %all-to-all-start = ((s32[16,8,128]{2,1,0:T(8,128)}), s32[16,8,128]{2,1,0:T(8,128)S(1)}, u32[]{:S(2)}, u32[]{:S(2)}) async-start(s32[16,8,128]{2,1,0:T(8,128)} %bitcast.6), calls=%async_computation | async-start | bytes 131072 | tf_op jit(solution)/shard_map/all_to_all | solution.py:435
  8.7 3.5 %shard_map.68.refs_1_ = f32[16,9,8,128]{3,2,1,0:T(8,128)} custom-call(f32[14,16384]{1,0:T(8,128)} %params_ref.3), custom_call_target="tpu_custom_call" | custom-call | tf_op jit(solution)/shard_map/pallas_call | solution.py:438
  12.2 1.6 all-to-all-done.refs_0_.index_ref
  13.8 0.6 copy-done.2
  14.4 17.5 %shard_map.69 = f32[16,9,8,128]{3,2,1,0:T(8,128)} custom-call(s32[16,8,128]{2,1,0:T(8,128)} %copy-done.2, f32[16,9,8,128]{3,2,1,0:T(8,128)} %shard_map.68.refs_1_), custom_call_target="tpu_custom_call" | custom-call | tf_op jit(solution)/shard_map/pallas_call | solution.py:428
  32.0 5.5 %all-to-all-start.1 = ((f32[16,9,8,128]{3,2,1,0:T(8,128)}), f32[16,9,8,128]{3,2,1,0:T(8,128)S(1)}, u32[]{:S(2)}, u32[]{:S(2)}) async-start(f32[16,9,8,128]{3,2,1,0:T(8,128)} %shard_map.69), calls=%async_computation.1 | async-start | bytes 1179648 | tf_op jit(solution)/shard_map/all_to_all | solution.py:415
  37.4 0.7 copy.12.upstream_ref
  38.1 0.1 copy-done.3
  38.3 0.2 reshape.17
  38.5 0.4 copy.10
  38.8 0.8 copy.11.refs_0_.index_ref
  39.7 6.5 %shard_map.73.refs_0_ = s32[16,8,128]{2,1,0:T(8,128)} custom-call(s32[16,8,128]{2,1,0:T(8,128)} %copy.11.refs_0_.index_ref), custom_call_target="tpu_custom_call" | custom-call | tf_op jit(solution)/shard_map/pallas_call | solution.py:421
  46.2 6.8 %all-to-all-done.1.refs_1_ = f32[16,9,8,128]{3,2,1,0:T(8,128)S(1)} async-done(((f32[16,9,8,128]{3,2,1,0:T(8,128)}), f32[16,9,8,128]{3,2,1,0:T(8,128)S(1)}, u32[]{:S(2)}, u32[]{:S(2)}) %all-to-all-start.1) | async-done | bytes 589856 | tf_op jit(solution)/shard_map/all_to_all | solution.py:415
  53.0 0.8 copy-done
  53.8 17.6 %shard_map.70.slots_ref = f32[16,9,8,128]{3,2,1,0:T(8,128)} custom-call(s32[16,8,128]{2,1,0:T(8,128)} %copy.11.refs_0_.index_ref, f32[16,9,8,128]{3,2,1,0:T(8,128)} %copy-done), custom_call_target="tpu_custom_call" | custom-call | tf_op jit(solution)/shard_map/pallas_call | solution.py:428
  71.4 37.2 %shard_map.71 = (f32[16,3,256]{2,1,0:T(4,128)}, f32[16,9,8,128]{3,2,1,0:T(8,128)}) custom-call(s32[16]{0:T(128)} %count_ref.1, s32[1]{0:T(128)} %bitcast.first_ref, f32[16,9,8,128]{3,2,1,0:T(8,128)} %shard_map.70.slots_ref, f32[16,3,256]{2,1,0:T(4,128)} %copy.12.upstream_ref), custom_call_target="tpu_custom_call" | custom-call | tf_op jit(solution)/shard_map/pallas_call | solution.py:456
  108.5 15.3 %shard_map.74 = f32[16,9,8,128]{3,2,1,0:T(8,128)} custom-call(s32[16,8,128]{2,1,0:T(8,128)} %shard_map.73.refs_0_, f32[16,9,8,128]{3,2,1,0:T(8,128)} %get-tuple-element.5.refs_1_), custom_call_target="tpu_custom_call" | custom-call | tf_op jit(solution)/shard_map/pallas_call | solution.py:428
  123.8 45.6 %all-to-all-start.2 = ((f32[16,9,8,128]{3,2,1,0:T(8,128)}), f32[16,9,8,128]{3,2,1,0:T(8,128)S(1)}, u32[]{:S(2)}, u32[]{:S(2)}) async-start(f32[16,9,8,128]{3,2,1,0:T(8,128)} %shard_map.74), calls=%async_computation.2 | async-start | bytes 1179648 | tf_op jit(solution)/shard_map/all_to_all | solution.py:415
  169.4 6.6 %shard_map.72.index_ref = s32[16,8,128]{2,1,0:T(8,128)} custom-call(s32[16,8,128]{2,1,0:T(8,128)} %copy-done.2), custom_call_target="tpu_custom_call" | custom-call | tf_op jit(solution)/shard_map/pallas_call | solution.py:421
  176.0 0.6 copy.14
  176.6 8.3 %all-to-all-done.2.grads_ref = f32[16,9,8,128]{3,2,1,0:T(8,128)S(1)} async-done(((f32[16,9,8,128]{3,2,1,0:T(8,128)}), f32[16,9,8,128]{3,2,1,0:T(8,128)S(1)}, u32[]{:S(2)}, u32[]{:S(2)}) %all-to-all-start.2) | async-done | bytes 589856 | tf_op jit(solution)/shard_map/all_to_all | solution.py:415
  185.0 0.8 copy-done.1
  185.8 18.3 %shard_map.75 = f32[14,16384]{1,0:T(8,128)} custom-call(s32[16,8,128]{2,1,0:T(8,128)} %shard_map.72.index_ref, f32[16,9,8,128]{3,2,1,0:T(8,128)} %copy-done.1, f32[14,16384]{1,0:T(8,128)} %params_ref.3), custom_call_target="tpu_custom_call" | custom-call | tf_op jit(solution)/shard_map/pallas_call | solution.py:488
  (8 shorter events, 0.0 us)
Async XLA Ops:
  2.1 11.7 %all-to-all-start = ((s32[16,8,128]{2,1,0:T(8,128)}), s32[16,8,128]{2,1,0:T(8,128)S(1)}, u32[]{:S(2)}, u32[]{:S(2)}) async-start(s32[16,8,128]{2,1,0:T(8,128)} %bitcast.6), calls=%async_computation | async-start | bytes 131072 | tf_op jit(solution)/shard_map/all_to_all | solution.py:435
  13.8 0.6 copy-start.2
  32.0 5.5 %copy-start.5 = (f32[16,3,256]{2,0,1:T(8,128)S(1)}, f32[16,3,256]{2,0,1:T(8,128)}, u32[]{:S(2)}) copy-start(f32[16,3,256]{2,0,1:T(8,128)} %param.9) | copy-start | bytes 147460
  32.0 21.0 %all-to-all-start.1 = ((f32[16,9,8,128]{3,2,1,0:T(8,128)}), f32[16,9,8,128]{3,2,1,0:T(8,128)S(1)}, u32[]{:S(2)}, u32[]{:S(2)}) async-start(f32[16,9,8,128]{3,2,1,0:T(8,128)} %shard_map.69), calls=%async_computation.1 | async-start | bytes 1179648 | tf_op jit(solution)/shard_map/all_to_all | solution.py:415
  37.4 0.8 copy-start.3
  53.0 0.8 copy-start
  123.8 61.1 %all-to-all-start.2 = ((f32[16,9,8,128]{3,2,1,0:T(8,128)}), f32[16,9,8,128]{3,2,1,0:T(8,128)S(1)}, u32[]{:S(2)}, u32[]{:S(2)}) async-start(f32[16,9,8,128]{3,2,1,0:T(8,128)} %shard_map.74), calls=%async_computation.2 | async-start | bytes 1179648 | tf_op jit(solution)/shard_map/all_to_all | solution.py:415
  169.4 6.6 %copy-start.4 = (f32[16,3,256]{2,1,0:T(4,128)S(1)}, f32[16,3,256]{2,1,0:T(4,128)}, u32[]{:S(2)}) copy-start(f32[16,3,256]{2,1,0:T(4,128)} %get-tuple-element.8) | copy-start | bytes 147460
  185.0 0.8 copy-start.1

commit v2 on v1

--- a/solution.py
+++ b/solution.py
@@ -12,6 +12,7 @@
 CHAN = 9
 PARAMS = 14
 FINE = 5
+WIDE = 4
 
 focal = 1000.0
 center_u = 512.0
@@ -236,6 +237,11 @@
     return head, (value - head.astype(f32)).astype(bf16)
 
 
+def split_stack(values):
+    both = [two_rows(value) for value in values]
+    return jnp.concatenate([head for head, _ in both] + [tail for _, tail in both], axis=0)
+
+
 def blend_kernel(
     count_ref,
     first_ref,
@@ -243,151 +249,197 @@
     upstream_ref,
     image_ref,
     grads_ref,
+    live,
     features,
     basis,
+    up_rows,
     alpha_s,
     gc_s,
-    weight_s,
     gain_s,
     offset_s,
-    pair,
+    image_s,
     moments,
     colour_grads,
 ):
-    t = pl.program_id(0)
-    tile = first_ref[0] + t
-    count = count_ref[t]
-    mid_u = ((tile % tile_row) * 16 + 8).astype(f32)
-    mid_v = ((tile // tile_row) * 16 + 8).astype(f32)
+    tiles, _, blocks, _ = slots_ref.shape
+    steps = BLOCK // ROWS
+    spare = tiles * blocks
     pixel = lax.broadcasted_iota(jnp.int32, (1, PIX), 1)
     x = (pixel & 15).astype(f32) - 7.5
     y = (pixel >> 4).astype(f32) - 7.5
     row = lax.broadcasted_iota(jnp.int32, (ROWS, PIX), 0)
-
-    @pl.when(t == 0)
-    def _():
-        basis[...] = jnp.zeros_like(basis)
-        features[...] = jnp.zeros_like(features)
-        for k in range(3):
-            for m, line in enumerate((jnp.ones_like(x), x, y, x * x, x * y, y * y)):
-                basis[6 * k + m : 6 * k + m + 1, 0:PIX] = line
-
-    monomials = jnp.concatenate(
-        [jnp.ones_like(x), x, y, x * x, x * y, y * y, jnp.zeros((2, PIX), f32)], axis=0
-    ).astype(bf16)
-    up = upstream_ref[0]
-    up_head = up.astype(bf16).astype(f32)
-    up_tail = up - up_head
-    basis[18:21, PIX:] = up_head
-    basis[21:24, PIX:] = up_tail
-    basis[24:27, PIX:] = up_head
-    basis16 = basis[...].astype(bf16)
-    up_both = jnp.concatenate([up_head, up_tail, jnp.zeros((2, PIX), f32)], axis=0).astype(bf16)
-
-    off_u = mid_u - slots_ref[0, 0]
-    off_v = mid_v - slots_ref[0, 1]
-    con_a, con_b, con_c = (slots_ref[0, 2], slots_ref[0, 3], slots_ref[0, 4])
-    log_op = jnp.maximum(jnp.log(slots_ref[0, 5]), log_floor)
-    side_u = con_a * off_u + con_b * off_v
-    side_v = con_b * off_u + con_c * off_v
-    coefs = [
-        log_op - 0.5 * (off_u * side_u + off_v * side_v),
-        -side_u,
-        -side_v,
-        -0.5 * con_a,
-        -con_b,
-        -0.5 * con_c,
-    ]
-    for m, coef in enumerate(coefs):
-        for k, part in enumerate(pieces(coef, 3)):
-            features[:, 6 * k + m, :] = part.astype(f32)
-    for c in range(3):
-        head, tail = two_rows(slots_ref[0, 6 + c])
-        features[:, 18 + c, :] = head.astype(f32)
-        features[:, 21 + c, :] = head.astype(f32)
-        features[:, 24 + c, :] = tail.astype(f32)
-    image_ref[...] = jnp.zeros_like(image_ref)
-    grads_ref[...] = jnp.zeros_like(grads_ref)
-    moments[...] = jnp.zeros_like(moments)
-    colour_grads[...] = jnp.zeros_like(colour_grads)
-
-    def forward(b, carry):
-        trans, image = carry
-        block = features[b]
-        both = lax.dot_general(
-            block.astype(bf16), basis16, (((0,), (0,)), ((), ())), preferred_element_type=f32
+    block_row = lax.broadcasted_iota(jnp.int32, (blocks, BLOCK), 0)
+    six = jnp.concatenate([jnp.ones_like(x), x, y, x * x, x * y, y * y], axis=0)
+    power_basis = jnp.concatenate([six, six, six, jnp.zeros((14, PIX), f32)], axis=0).astype(bf16)
+    monomials = jnp.concatenate([six, jnp.zeros((2, PIX), f32)], axis=0).astype(bf16)
+
+    def middle(t):
+        tile = first_ref[0] + t
+        return (
+            ((tile % tile_row) * 16 + 8).astype(f32),
+            ((tile // tile_row) * 16 + 8).astype(f32),
         )
-        prod = jnp.ones((ROWS, PIX), f32)
-        ahead = jnp.zeros((ROWS, PIX), f32)
-        local = []
-        for i in range(BLOCK // ROWS):
-            alpha = jnp.exp(both[i * ROWS : i * ROWS + ROWS, :PIX])
-            gc = both[i * ROWS : i * ROWS + ROWS, PIX:]
-            weight = prod * alpha
-            ahead = ahead + weight * gc
-            prod = prod - weight
-            alpha_s[b, i] = alpha
-            gc_s[b, i] = gc
-            local.append(weight)
-        gain_s[b] = prod
-        offset_s[b] = ahead
-        before, whole = scan_before(prod, row)
-        before = before * trans
-        heads, tails = [], []
-        for i in range(BLOCK // ROWS):
-            weight = local[i] * before
-            weight_s[b, i] = weight
-            head, tail = two_rows(weight)
-            heads.append(head)
-            tails.append(tail)
-        w2 = jnp.concatenate(heads + tails, axis=0)
-        head = block[18:21]
-        tail = block[24:27]
-        colour = jnp.concatenate(
-            [
-                jnp.concatenate([head, tail, jnp.zeros((2, BLOCK), f32)], axis=0),
-                jnp.concatenate([head, jnp.zeros((5, BLOCK), f32)], axis=0),
-            ],
-            axis=1,
-        ).astype(bf16)
-        image = image + jnp.dot(colour, w2, preferred_element_type=f32)
-        got = lax.dot_general(up_both, w2, (((1,), (1,)), ((), ())), preferred_element_type=f32)
-        colour_grads[:, b, :] = got[0:3, :BLOCK] + got[0:3, BLOCK:] + got[3:6, :BLOCK]
-        return (trans * whole, image)
-
-    _, image = lax.fori_loop(
-        0, count, forward, (jnp.ones((1, PIX), f32), jnp.zeros((ROWS, PIX), f32))
-    )
-    image_ref[0] = image[0:3] + image[3:6]
-
-    def backward(step, incoming):
-        b = count - 1 - step
-        behind, start = scan_behind(gain_s[b], offset_s[b], row, incoming)
-        heads, tails = [], []
-        for i in reversed(range(BLOCK // ROWS)):
-            diff = gc_s[b, i] - behind
-            head, tail = two_rows(weight_s[b, i] * diff)
-            heads.append(head)
-            tails.append(tail)
-            behind = behind + alpha_s[b, i] * diff
-        h2 = jnp.concatenate(heads[::-1] + tails[::-1], axis=0)
-        got = lax.dot_general(monomials, h2, (((1,), (1,)), ((), ())), preferred_element_type=f32)
-        moments[:, b, :] = got[:, :BLOCK] + got[:, BLOCK:]
-        return start
-
-    lax.fori_loop(0, count, backward, jnp.zeros((1, PIX), f32))
-
-    sum_h, sum_x, sum_y, sum_xx, sum_xy, sum_yy = [moments[m] for m in range(6)]
-    sum_u = sum_x + off_u * sum_h
-    sum_v = sum_y + off_v * sum_h
-    grads_ref[0, 0] = con_a * sum_u + con_b * sum_v
-    grads_ref[0, 1] = con_b * sum_u + con_c * sum_v
-    grads_ref[0, 2] = -0.5 * (sum_xx + off_u * (sum_x + sum_u))
-    grads_ref[0, 3] = -(sum_xy + off_v * sum_x + off_u * sum_v)
-    grads_ref[0, 4] = -0.5 * (sum_yy + off_v * (sum_y + sum_v))
-    grads_ref[0, 5] = sum_h
-    for c in range(3):
-        grads_ref[0, 6 + c] = colour_grads[c]
+
+    basis[...] = jnp.zeros_like(basis)
+    features[pl.ds(spare, 1)] = jnp.zeros((1, 32, BLOCK), f32)
+    features[:, 27:32, :] = jnp.zeros((spare + 1, 5, BLOCK), f32)
+    up_rows[pl.ds(tiles, 1)] = jnp.zeros((1, ROWS, PIX), f32)
+    image_s[...] = jnp.zeros_like(image_s)
+
+    def prepare(t, total):
+        up = upstream_ref[t]
+        up_head = up.astype(bf16).astype(f32)
+        up_tail = up - up_head
+        basis[t, 18:21, :] = up_head
+        basis[t, 21:24, :] = up_tail
+        basis[t, 24:27, :] = up_head
+        up_rows[t] = jnp.concatenate([up_head, up_tail, jnp.zeros((2, PIX), f32)], axis=0)
+        mid_u, mid_v = middle(t)
+        off_u = mid_u - slots_ref[t, 0]
+        off_v = mid_v - slots_ref[t, 1]
+        con_a, con_b, con_c = (slots_ref[t, 2], slots_ref[t, 3], slots_ref[t, 4])
+        log_op = jnp.maximum(jnp.log(slots_ref[t, 5]), log_floor)
+        side_u = con_a * off_u + con_b * off_v
+        side_v = con_b * off_u + con_c * off_v
+        coefs = [
+            log_op - 0.5 * (off_u * side_u + off_v * side_v),
+            -side_u,
+            -side_v,
+            -0.5 * con_a,
+            -con_b,
+            -0.5 * con_c,
+        ]
+        here = pl.ds(t * blocks, blocks)
+        for m, coef in enumerate(coefs):
+            for k, part in enumerate(pieces(coef, 3)):
+                features[here, 6 * k + m, :] = part.astype(f32)
+        for c in range(3):
+            head, tail = two_rows(slots_ref[t, 6 + c])
+            features[here, 18 + c, :] = head.astype(f32)
+            features[here, 21 + c, :] = head.astype(f32)
+            features[here, 24 + c, :] = tail.astype(f32)
+        for b in range(blocks):
+            live[total] = t * blocks + b
+            total = total + (b < count_ref[t]).astype(jnp.int32)
+        return total
+
+    total = lax.fori_loop(0, tiles, prepare, jnp.int32(0))
+    for k in range(WIDE):
+        live[total + k] = spare
+    rounds = (total + WIDE - 1) // WIDE
+
+    def local_pass(k, carry):
+        for w in range(WIDE):
+            name = live[k * WIDE + w]
+            block = features[name].astype(bf16)
+            power = lax.dot_general(
+                block, power_basis, (((0,), (0,)), ((), ())), preferred_element_type=f32
+            )
+            shade = lax.dot_general(
+                block,
+                basis[name // blocks].astype(bf16),
+                (((0,), (0,)), ((), ())),
+                preferred_element_type=f32,
+            )
+            prod = jnp.ones((ROWS, PIX), f32)
+            ahead = jnp.zeros((ROWS, PIX), f32)
+            for i in range(steps):
+                alpha = jnp.exp(power[i * ROWS : i * ROWS + ROWS])
+                gc = shade[i * ROWS : i * ROWS + ROWS]
+                weight = prod * alpha
+                ahead = ahead + weight * gc
+                prod = prod - weight
+                alpha_s[name, i] = alpha
+                gc_s[name, i] = gc
+            gain_s[name] = prod
+            offset_s[name] = ahead
+        return carry
+
+    lax.fori_loop(0, rounds, local_pass, 0)
+
+    def scan_pass(t, carry):
+        trans = jnp.ones((1, PIX), f32)
+        gains, offsets = [], []
+        for b in range(blocks):
+            name = t * blocks + b
+            alive = b < count_ref[t]
+            gains.append(jnp.where(alive, gain_s[name], 1.0))
+            offsets.append(jnp.where(alive, offset_s[name], 0.0))
+        for b in range(blocks):
+            before, whole = scan_before(gains[b], row)
+            gain_s[t * blocks + b] = before * trans
+            trans = trans * whole
+        incoming = jnp.zeros((1, PIX), f32)
+        for b in reversed(range(blocks)):
+            behind, incoming = scan_behind(gains[b], offsets[b], row, incoming)
+            offset_s[t * blocks + b] = behind
+        return carry
+
+    lax.fori_loop(0, tiles, scan_pass, 0)
+
+    def grad_pass(k, carry):
+        for w in range(WIDE):
+            name = live[k * WIDE + w]
+            t, b = name // blocks, name % blocks
+            prod = gain_s[name]
+            weights = []
+            for i in range(steps):
+                weight = prod * alpha_s[name, i]
+                prod = prod - weight
+                weights.append(weight)
+            behind = offset_s[name]
+            hits = []
+            for i in reversed(range(steps)):
+                diff = gc_s[name, i] - behind
+                hits.append(weights[i] * diff)
+                behind = behind + alpha_s[name, i] * diff
+            w2 = split_stack(weights)
+            h2 = split_stack(hits[::-1])
+            head = features[name, 18:21]
+            tail = features[name, 24:27]
+            colour = jnp.concatenate(
+                [
+                    jnp.concatenate([head, tail, jnp.zeros((2, BLOCK), f32)], axis=0),
+                    jnp.concatenate([head, jnp.zeros((5, BLOCK), f32)], axis=0),
+                ],
+                axis=1,
+            ).astype(bf16)
+            image_s[t] += jnp.dot(colour, w2, preferred_element_type=f32)
+            got = lax.dot_general(
+                up_rows[t].astype(bf16), w2, (((1,), (1,)), ((), ())), preferred_element_type=f32
+            )
+            colour_grads[t, :, b, :] = got[0:3, :BLOCK] + got[0:3, BLOCK:] + got[3:6, :BLOCK]
+            got = lax.dot_general(
+                monomials, h2, (((1,), (1,)), ((), ())), preferred_element_type=f32
+            )
+            moments[t, :, b, :] = got[:, :BLOCK] + got[:, BLOCK:]
+        return carry
+
+    lax.fori_loop(0, rounds, grad_pass, 0)
+
+    def finish(t, carry):
+        image_ref[t] = image_s[t, 0:3] + image_s[t, 3:6]
+        alive = block_row < count_ref[t]
+        sum_h, sum_x, sum_y, sum_xx, sum_xy, sum_yy = [
+            jnp.where(alive, moments[t, m], 0.0) for m in range(6)
+        ]
+        mid_u, mid_v = middle(t)
+        off_u = mid_u - slots_ref[t, 0]
+        off_v = mid_v - slots_ref[t, 1]
+        con_a, con_b, con_c = (slots_ref[t, 2], slots_ref[t, 3], slots_ref[t, 4])
+        sum_u = sum_x + off_u * sum_h
+        sum_v = sum_y + off_v * sum_h
+        grads_ref[t, 0] = con_a * sum_u + con_b * sum_v
+        grads_ref[t, 1] = con_b * sum_u + con_c * sum_v
+        grads_ref[t, 2] = -0.5 * (sum_xx + off_u * (sum_x + sum_u))
+        grads_ref[t, 3] = -(sum_xy + off_v * sum_x + off_u * sum_v)
+        grads_ref[t, 4] = -0.5 * (sum_yy + off_v * (sum_y + sum_v))
+        grads_ref[t, 5] = sum_h
+        for c in range(3):
+            grads_ref[t, 6 + c] = jnp.where(alive, colour_grads[t, c], 0.0)
+        return carry
+
+    lax.fori_loop(0, tiles, finish, 0)
 
 
 def params(**kw):
@@ -453,34 +505,31 @@
     slots_in = gather(order, arrived, FINE)
     first_tile = (lax.axis_index("tile") * tiles_here).reshape(1).astype(jnp.int32)
     steps = BLOCK // ROWS
+    spare = tiles_here * blocks
     image, slot_grads = pl.pallas_call(
         blend_kernel,
-        grid=(tiles_here,),
         in_specs=[
             pl.BlockSpec(memory_space=pltpu.SMEM),
             pl.BlockSpec(memory_space=pltpu.SMEM),
-            pl.BlockSpec((1, CHAN, blocks, BLOCK), lambda t: (t, 0, 0, 0)),
-            pl.BlockSpec((1, 3, PIX), lambda t: (t, 0, 0)),
-        ],
-        out_specs=[
-            pl.BlockSpec((1, 3, PIX), lambda t: (t, 0, 0)),
-            pl.BlockSpec((1, CHAN, blocks, BLOCK), lambda t: (t, 0, 0, 0)),
+            pl.BlockSpec(memory_space=pltpu.VMEM),
+            pl.BlockSpec(memory_space=pltpu.VMEM),
         ],
         out_shape=[
             jax.ShapeDtypeStruct((tiles_here, 3, PIX), f32),
             jax.ShapeDtypeStruct((tiles_here, CHAN, blocks, BLOCK), f32),
         ],
         scratch_shapes=[
-            pltpu.VMEM((blocks, 32, BLOCK), f32),
-            pltpu.VMEM((32, 2 * PIX), f32),
-            pltpu.VMEM((blocks, steps, ROWS, PIX), f32),
-            pltpu.VMEM((blocks, steps, ROWS, PIX), f32),
-            pltpu.VMEM((blocks, steps, ROWS, PIX), f32),
-            pltpu.VMEM((blocks, ROWS, PIX), f32),
-            pltpu.VMEM((blocks, ROWS, PIX), f32),
-            pltpu.VMEM((8, 128), f32),
-            pltpu.VMEM((8, blocks, BLOCK), f32),
-            pltpu.VMEM((3, blocks, BLOCK), f32),
+            pltpu.SMEM((spare + WIDE,), jnp.int32),
+            pltpu.VMEM((spare + 1, 32, BLOCK), f32),
+            pltpu.VMEM((tiles_here + 1, 32, PIX), f32),
+            pltpu.VMEM((tiles_here + 1, ROWS, PIX), f32),
+            pltpu.VMEM((spare + 1, steps, ROWS, PIX), f32),
+            pltpu.VMEM((spare + 1, steps, ROWS, PIX), f32),
+            pltpu.VMEM((spare + 1, ROWS, PIX), f32),
+            pltpu.VMEM((spare + 1, ROWS, PIX), f32),
+            pltpu.VMEM((tiles_here + 1, ROWS, PIX), f32),
+            pltpu.VMEM((tiles_here + 1, ROWS, blocks, BLOCK), f32),
+            pltpu.VMEM((tiles_here + 1, 3, blocks, BLOCK), f32),
         ],
         compiler_params=params(),
     )(block_count, first_tile, slots_in, image_grad)

time: 200 us -> 154 us (0.77)
  the two profiles are of different devices: /device:TPU:11 before, /device:TPU:0 now
where the time goes in v2:
time: 154 us; the launch traced here: 153 us
  Pallas kernels  106 us (69%)
  starting transfers between devices  22 us (14%)
  waiting for transfers between devices  18.5 us (12%)
  local copies, waits for them, and re-layouts  6.59 us (4%)
    pallas_call x3, Pallas kernels, gather(): pl.pallas_call(lambda *refs: gather_kernel(fine, *refs), out_shape=jax.Sh...  50.4 us
    pallas_call x1, Pallas kernels, local(): pl.pallas_call(blend_kernel, in_specs=[pl.BlockSpec(memory_space=pltpu.SM...  20.3 us
    pallas_call x1, Pallas kernels, local(): pl.pallas_call(return_kernel, out_shape=jax.ShapeDtypeStruct(gauss_params...  18.3 us
    all_to_all x2, waiting for transfers between devices, exchange(): lax.all_to_all(value, 'tile', split_axis=0, concat_axis=0, tiled=True)  15.1 us
    all_to_all x2, starting transfers between devices, exchange(): lax.all_to_all(value, 'tile', split_axis=0, concat_axis=0, tiled=True)  14.6 us
    pallas_call x2, Pallas kernels, invert(): pl.pallas_call(invert_kernel, out_shape=jax.ShapeDtypeStruct(index_shape,...  13.1 us
    all_to_all x1, starting transfers between devices, local(): lax.all_to_all(wanted.reshape(peers, lines, LANES), 'tile', split_axis=0,...  7.39 us
    unnamed x15, local copies, waits for them, and re-layouts  5.21 us
  transfers between devices with their start and end apart: 3, of which 3 were waited for; matrix products, arithmetic and copies ran while one was open for 2% of the time, Pallas kernels for 11%

profile of v2, /device:TPU:0, one launch (start us, length us, event | category | flops | bytes accessed | tf_op | source)
XLA Modules:
  0.0 153.4 jit_solution(5690789700114712324)
XLA Ops:
  0.6 1.5 copy.15
  2.1 7.4 %all-to-all-start = ((s32[16,8,128]{2,1,0:T(8,128)}), s32[16,8,128]{2,1,0:T(8,128)S(1)}, u32[]{:S(2)}, u32[]{:S(2)}) async-start(s32[16,8,128]{2,1,0:T(8,128)} %bitcast.6), calls=%async_computation | async-start | bytes 131072 | tf_op jit(solution)/shard_map/all_to_all | solution.py:487
  9.5 3.5 %shard_map.68.refs_1_ = f32[16,9,8,128]{3,2,1,0:T(8,128)} custom-call(f32[14,16384]{1,0:T(8,128)} %params_ref.3), custom_call_target="tpu_custom_call" | custom-call | tf_op jit(solution)/shard_map/pallas_call | solution.py:490
  13.0 3.4 %all-to-all-done.refs_0_.index_ref = s32[16,8,128]{2,1,0:T(8,128)S(1)} async-done(((s32[16,8,128]{2,1,0:T(8,128)}), s32[16,8,128]{2,1,0:T(8,128)S(1)}, u32[]{:S(2)}, u32[]{:S(2)}) %all-to-all-start) | async-done | bytes 65568 | tf_op jit(solution)/shard_map/all_to_all | solution.py:487
  16.4 0.6 copy-done.2
  17.0 17.5 %shard_map.69 = f32[16,9,8,128]{3,2,1,0:T(8,128)} custom-call(s32[16,8,128]{2,1,0:T(8,128)} %copy-done.2, f32[16,9,8,128]{3,2,1,0:T(8,128)} %shard_map.68.refs_1_), custom_call_target="tpu_custom_call" | custom-call | tf_op jit(solution)/shard_map/pallas_call | solution.py:480
  34.6 3.7 %all-to-all-start.1 = ((f32[16,9,8,128]{3,2,1,0:T(8,128)}), f32[16,9,8,128]{3,2,1,0:T(8,128)S(1)}, u32[]{:S(2)}, u32[]{:S(2)}) async-start(f32[16,9,8,128]{3,2,1,0:T(8,128)} %shard_map.69), calls=%async_computation.1 | async-start | bytes 1179648 | tf_op jit(solution)/shard_map/all_to_all | solution.py:467
  38.3 0.7 copy.12.upstream_ref
  39.0 0.1 copy-done.3
  39.1 0.2 reshape.17
  39.4 0.4 copy.10
  39.7 0.8 copy.11.refs_0_.index_ref
  40.5 6.5 %shard_map.73.refs_0_ = s32[16,8,128]{2,1,0:T(8,128)} custom-call(s32[16,8,128]{2,1,0:T(8,128)} %copy.11.refs_0_.index_ref), custom_call_target="tpu_custom_call" | custom-call | tf_op jit(solution)/shard_map/pallas_call | solution.py:473
  47.1 6.7 %all-to-all-done.1.refs_1_ = f32[16,9,8,128]{3,2,1,0:T(8,128)S(1)} async-done(((f32[16,9,8,128]{3,2,1,0:T(8,128)}), f32[16,9,8,128]{3,2,1,0:T(8,128)S(1)}, u32[]{:S(2)}, u32[]{:S(2)}) %all-to-all-start.1) | async-done | bytes 589856 | tf_op jit(solution)/shard_map/all_to_all | solution.py:467
  53.8 0.8 copy-done
  54.6 17.5 %shard_map.70.slots_ref = f32[16,9,8,128]{3,2,1,0:T(8,128)} custom-call(s32[16,8,128]{2,1,0:T(8,128)} %copy.11.refs_0_.index_ref, f32[16,9,8,128]{3,2,1,0:T(8,128)} %copy-done), custom_call_target="tpu_custom_call" | custom-call | tf_op jit(solution)/shard_map/pallas_call | solution.py:480
  72.2 20.3 %shard_map.71 = (f32[16,3,256]{2,1,0:T(4,128)}, f32[16,9,8,128]{3,2,1,0:T(8,128)}) custom-call(s32[16]{0:T(128)} %count_ref.1, s32[1]{0:T(128)} %bitcast.first_ref, f32[16,9,8,128]{3,2,1,0:T(8,128)} %shard_map.70.slots_ref, f32[16,3,256]{2,1,0:T(4,128)} %copy.12.upstream_ref), custom_call_target="tpu_custom_call" | custom-call | tf_op jit(solution)/shard_map/pallas_call | solution.py:509
  92.5 15.3 %shard_map.74 = f32[16,9,8,128]{3,2,1,0:T(8,128)} custom-call(s32[16,8,128]{2,1,0:T(8,128)} %shard_map.73.refs_0_, f32[16,9,8,128]{3,2,1,0:T(8,128)} %get-tuple-element.5.refs_1_), custom_call_target="tpu_custom_call" | custom-call | tf_op jit(solution)/shard_map/pallas_call | solution.py:480
  107.8 10.9 %all-to-all-start.2 = ((f32[16,9,8,128]{3,2,1,0:T(8,128)}), f32[16,9,8,128]{3,2,1,0:T(8,128)S(1)}, u32[]{:S(2)}, u32[]{:S(2)}) async-start(f32[16,9,8,128]{3,2,1,0:T(8,128)} %shard_map.74), calls=%async_computation.2 | async-start | bytes 1179648 | tf_op jit(solution)/shard_map/all_to_all | solution.py:467
  118.8 6.6 %shard_map.72.index_ref = s32[16,8,128]{2,1,0:T(8,128)} custom-call(s32[16,8,128]{2,1,0:T(8,128)} %copy-done.2), custom_call_target="tpu_custom_call" | custom-call | tf_op jit(solution)/shard_map/pallas_call | solution.py:473
  125.3 0.6 copy.14
  126.0 8.3 %all-to-all-done.2.grads_ref = f32[16,9,8,128]{3,2,1,0:T(8,128)S(1)} async-done(((f32[16,9,8,128]{3,2,1,0:T(8,128)}), f32[16,9,8,128]{3,2,1,0:T(8,128)S(1)}, u32[]{:S(2)}, u32[]{:S(2)}) %all-to-all-start.2) | async-done | bytes 589856 | tf_op jit(solution)/shard_map/all_to_all | solution.py:467
  134.3 0.8 copy-done.1
  135.1 18.3 %shard_map.75 = f32[14,16384]{1,0:T(8,128)} custom-call(s32[16,8,128]{2,1,0:T(8,128)} %shard_map.72.index_ref, f32[16,9,8,128]{3,2,1,0:T(8,128)} %copy-done.1, f32[14,16384]{1,0:T(8,128)} %params_ref.3), custom_call_target="tpu_custom_call" | custom-call | tf_op jit(solution)/shard_map/pallas_call | solution.py:537
  (8 shorter events, 0.0 us)
Async XLA Ops:
  2.1 14.3 %all-to-all-start = ((s32[16,8,128]{2,1,0:T(8,128)}), s32[16,8,128]{2,1,0:T(8,128)S(1)}, u32[]{:S(2)}, u32[]{:S(2)}) async-start(s32[16,8,128]{2,1,0:T(8,128)} %bitcast.6), calls=%async_computation | async-start | bytes 131072 | tf_op jit(solution)/shard_map/all_to_all | solution.py:487
  16.4 0.6 copy-start.2
  34.6 3.7 %copy-start.5 = (f32[16,3,256]{2,0,1:T(8,128)S(1)}, f32[16,3,256]{2,0,1:T(8,128)}, u32[]{:S(2)}) copy-start(f32[16,3,256]{2,0,1:T(8,128)} %param.9) | copy-start | bytes 147460
  34.6 19.2 %all-to-all-start.1 = ((f32[16,9,8,128]{3,2,1,0:T(8,128)}), f32[16,9,8,128]{3,2,1,0:T(8,128)S(1)}, u32[]{:S(2)}, u32[]{:S(2)}) async-start(f32[16,9,8,128]{3,2,1,0:T(8,128)} %shard_map.69), calls=%async_computation.1 | async-start | bytes 1179648 | tf_op jit(solution)/shard_map/all_to_all | solution.py:467
  38.3 0.8 copy-start.3
  53.8 0.8 copy-start
  107.8 26.5 %all-to-all-start.2 = ((f32[16,9,8,128]{3,2,1,0:T(8,128)}), f32[16,9,8,128]{3,2,1,0:T(8,128)S(1)}, u32[]{:S(2)}, u32[]{:S(2)}) async-start(f32[16,9,8,128]{3,2,1,0:T(8,128)} %shard_map.74), calls=%async_computation.2 | async-start | bytes 1179648 | tf_op jit(solution)/shard_map/all_to_all | solution.py:467
  118.7 6.6 %copy-start.4 = (f32[16,3,256]{2,1,0:T(4,128)S(1)}, f32[16,3,256]{2,1,0:T(4,128)}, u32[]{:S(2)}) copy-start(f32[16,3,256]{2,1,0:T(4,128)} %get-tuple-element.8) | copy-start | bytes 147460
  134.3 0.8 copy-start.1

commit v3 on v2

--- a/solution.py
+++ b/solution.py
@@ -11,8 +11,9 @@
 ROWS = 8
 CHAN = 9
 PARAMS = 14
-FINE = 5
-WIDE = 4
+LANED = 3
+FINE = 2
+WIDE = 8
 
 focal = 1000.0
 center_u = 512.0
@@ -37,8 +38,8 @@
 
 
 def fill_table(read, table, table_low, fine):
-    for c in range(CHAN):
-        wide = jnp.concatenate([read(c, 0), read(c, 1)], axis=1)
+    for c in range(CHAN - LANED):
+        wide = jnp.concatenate([read(LANED + c, 0), read(LANED + c, 1)], axis=1)
         part = pieces(wide, 3 if c < fine else 2)
         rows = pl.ds(c * 64, 64)
         table[rows, 0:256] = part[0]
@@ -50,8 +51,9 @@
 def pick(index, table, table_low, fine):
     column = (index & 127) | ((index >> 13) << 7)
     row = (index >> 7) & 63
-    places = lax.broadcasted_iota(jnp.int32, (256, 256), 0)
-    chosen = (jnp.broadcast_to(column, (256, 256)) == places).astype(f32).astype(bf16)
+    places = lax.broadcasted_iota(jnp.int32, (256, 256), 0).astype(f32).astype(bf16)
+    column = jnp.broadcast_to(column.astype(f32).astype(bf16), (256, 256))
+    chosen = jnp.where(column == places, bf16(1), bf16(0))
     row_hit = jnp.broadcast_to(row, (64, 256)) == lax.broadcasted_iota(jnp.int32, (64, 256), 0)
     both = jnp.dot(
         table[...], jnp.concatenate([chosen, chosen], axis=0), preferred_element_type=f32
@@ -59,7 +61,7 @@
     if fine:
         low = jnp.dot(table_low[...], chosen, preferred_element_type=f32)
     out = []
-    for c in range(CHAN):
+    for c in range(CHAN - LANED):
         mine = both[c * 64 : c * 64 + 64]
         if c < fine:
             mine = mine + low[c * 64 : c * 64 + 64]
@@ -67,16 +69,33 @@
     return out
 
 
-def gather_all(index_ref, out_ref, table, table_low, fine):
+def gather_all(index_ref, in_ref, out_ref, table, table_low, fine):
+    groups = in_ref.shape[0]
+    fill_table(lambda c, half: read_half(in_ref, c, half), table, table_low, fine)
+
     def step(t, carry):
+        whole = index_ref[t]
+        row, column = whole >> 7, whole & 127
+        found = [jnp.zeros((ROWS, LANES), f32) for _ in range(LANED)]
+        quarter = groups // (ROWS // 2)
         for half in range(ROWS // 2):
+            for q in range(half * quarter, half * quarter + quarter):
+                for s in range(ROWS):
+                    hit = row == q * ROWS + s
+                    for c in range(LANED):
+                        line = jnp.broadcast_to(in_ref[q, c, s : s + 1, :], (ROWS, LANES))
+                        found[c] = jnp.where(
+                            hit, jnp.take_along_axis(line, column, axis=1), found[c]
+                        )
             index = jnp.concatenate(
                 [index_ref[t, 2 * half : 2 * half + 1, :], index_ref[t, 2 * half + 1 : 2 * half + 2, :]],
                 axis=1,
             )
             for c, line in enumerate(pick(index, table, table_low, fine)):
-                out_ref[t, c, 2 * half : 2 * half + 1, :] = line[:, :LANES]
-                out_ref[t, c, 2 * half + 1 : 2 * half + 2, :] = line[:, LANES:]
+                out_ref[t, LANED + c, 2 * half : 2 * half + 1, :] = line[:, :LANES]
+                out_ref[t, LANED + c, 2 * half + 1 : 2 * half + 2, :] = line[:, LANES:]
+        for c in range(LANED):
+            out_ref[t, c] = found[c]
         return carry
 
     lax.fori_loop(0, index_ref.shape[0], step, 0)
@@ -189,13 +208,11 @@
 
 
 def gather_kernel(fine, index_ref, in_ref, out_ref, table, table_low):
-    fill_table(lambda c, half: read_half(in_ref, c, half), table, table_low, fine)
-    gather_all(index_ref, out_ref, table, table_low, fine)
+    gather_all(index_ref, in_ref, out_ref, table, table_low, fine)
 
 
 def return_kernel(index_ref, grads_ref, params_ref, out_ref, table, table_low, summed, raw, stage):
-    fill_table(lambda c, half: read_half(grads_ref, c, half), table, table_low, 0)
-    gather_all(index_ref, summed, table, table_low, 0)
+    gather_all(index_ref, grads_ref, summed, table, table_low, 0)
 
     def step(t, carry):
         for s in range(ROWS):
@@ -245,9 +262,15 @@
 def blend_kernel(
     count_ref,
     first_ref,
-    slots_ref,
+    order_ref,
+    back_ref,
+    arrived_ref,
     upstream_ref,
     image_ref,
+    sent_ref,
+    table,
+    table_low,
+    slots_ref,
     grads_ref,
     live,
     features,
@@ -261,6 +284,7 @@
     moments,
     colour_grads,
 ):
+    gather_all(order_ref, arrived_ref, slots_ref, table, table_low, FINE)
     tiles, _, blocks, _ = slots_ref.shape
     steps = BLOCK // ROWS
     spare = tiles * blocks
@@ -440,6 +464,7 @@
         return carry
 
     lax.fori_loop(0, tiles, finish, 0)
+    gather_all(back_ref, grads_ref, sent_ref, table, table_low, 0)
 
 
 def params(**kw):
@@ -457,7 +482,7 @@
     shape = (groups, CHAN, ROWS, LANES)
     index_shape = (groups, ROWS, LANES)
     tables = [
-        pltpu.VMEM((CHAN * 64, 512), bf16),
+        pltpu.VMEM(((CHAN - LANED) * 64, 512), bf16),
         pltpu.VMEM((FINE * 64, 256), bf16),
     ]
 
@@ -502,23 +527,27 @@
     outgoing = gather(asked, projected, FINE)
     arrived = exchange(outgoing)
     asked_back = invert(asked)
-    slots_in = gather(order, arrived, FINE)
     first_tile = (lax.axis_index("tile") * tiles_here).reshape(1).astype(jnp.int32)
     steps = BLOCK // ROWS
     spare = tiles_here * blocks
-    image, slot_grads = pl.pallas_call(
+    image, sent = pl.pallas_call(
         blend_kernel,
         in_specs=[
             pl.BlockSpec(memory_space=pltpu.SMEM),
             pl.BlockSpec(memory_space=pltpu.SMEM),
             pl.BlockSpec(memory_space=pltpu.VMEM),
             pl.BlockSpec(memory_space=pltpu.VMEM),
+            pl.BlockSpec(memory_space=pltpu.VMEM),
+            pl.BlockSpec(memory_space=pltpu.VMEM),
         ],
         out_shape=[
             jax.ShapeDtypeStruct((tiles_here, 3, PIX), f32),
-            jax.ShapeDtypeStruct((tiles_here, CHAN, blocks, BLOCK), f32),
-        ],
-        scratch_shapes=[
+            jax.ShapeDtypeStruct(shape, f32),
+        ],
+        scratch_shapes=tables
+        + [
+            pltpu.VMEM((tiles_here, CHAN, blocks, BLOCK), f32),
+            pltpu.VMEM((tiles_here, CHAN, blocks, BLOCK), f32),
             pltpu.SMEM((spare + WIDE,), jnp.int32),
             pltpu.VMEM((spare + 1, 32, BLOCK), f32),
             pltpu.VMEM((tiles_here + 1, 32, PIX), f32),
@@ -532,8 +561,8 @@
             pltpu.VMEM((tiles_here + 1, 3, blocks, BLOCK), f32),
         ],
         compiler_params=params(),
-    )(block_count, first_tile, slots_in, image_grad)
-    returned = exchange(gather(order_back, slot_grads, 0))
+    )(block_count, first_tile, order, order_back, arrived, image_grad)
+    returned = exchange(sent)
     param_grads = pl.pallas_call(
         return_kernel,
         out_shape=jax.ShapeDtypeStruct(gauss_params.shape, f32),

time: 154 us -> 130 us (0.84)
  Pallas kernels: 106 us -> 88 us
  starting transfers between devices: 22 us -> 15.6 us
    pallas_call x3 -> x1, Pallas kernels: 50.4 us -> 13.1 us  [gather(): pl.pallas_call(lambda *refs: gather_kernel(fine, *refs), out_shape=jax.Sh...]
    pallas_call x1, Pallas kernels: 20.3 us -> 43.5 us  [local(): pl.pallas_call(blend_kernel, in_specs=[pl.BlockSpec(memory_space=pltpu.SM...]
    all_to_all x2, starting transfers between devices: 14.6 us -> 8.18 us  [exchange(): lax.all_to_all(value, 'tile', split_axis=0, concat_axis=0, tiled=True)]
    pallas_call x1, Pallas kernels: 18.3 us -> 14.9 us  [local(): pl.pallas_call(return_kernel, out_shape=jax.ShapeDtypeStruct(gauss_params...]
  transfers between devices with their start and end apart: 3 -> 3, of which waited for: 3 -> 3; matrix products, arithmetic and copies ran while one was open for 2% -> 2% of each run, Pallas kernels for 11% -> 13%
where the time goes in v3:
time: 130 us; the launch traced here: 129 us
  Pallas kernels  88 us (68%)
  waiting for transfers between devices  18.5 us (14%)
  starting transfers between devices  15.6 us (12%)
  local copies, waits for them, and re-layouts  6.59 us (5%)
    pallas_call x1, Pallas kernels, local(): pl.pallas_call(blend_kernel, in_specs=[pl.BlockSpec(memory_space=pltpu.SM...  43.5 us
    all_to_all x2, waiting for transfers between devices, exchange(): lax.all_to_all(value, 'tile', split_axis=0, concat_axis=0, tiled=True)  15.1 us
    pallas_call x1, Pallas kernels, local(): pl.pallas_call(return_kernel, out_shape=jax.ShapeDtypeStruct(gauss_params...  14.9 us
    pallas_call x2, Pallas kernels, invert(): pl.pallas_call(invert_kernel, out_shape=jax.ShapeDtypeStruct(index_shape,...  13.1 us
    pallas_call x1, Pallas kernels, gather(): pl.pallas_call(lambda *refs: gather_kernel(fine, *refs), out_shape=jax.Sh...  13.1 us
    all_to_all x2, starting transfers between devices, exchange(): lax.all_to_all(value, 'tile', split_axis=0, concat_axis=0, tiled=True)  8.18 us
    all_to_all x1, starting transfers between devices, local(): lax.all_to_all(wanted.reshape(peers, lines, LANES), 'tile', split_axis=0,...  7.39 us
    unnamed x15, local copies, waits for them, and re-layouts  5.21 us
  transfers between devices with their start and end apart: 3, of which 3 were waited for; matrix products, arithmetic and copies ran while one was open for 2% of the time, Pallas kernels for 13%

profile of v3, /device:TPU:0, one launch (start us, length us, event | category | flops | bytes accessed | tf_op | source)
XLA Modules:
  0.0 129.4 jit_solution(6974067593117315467)
XLA Ops:
  0.6 1.5 %copy.15 = s32[2,8,8,128]{3,2,1,0:T(8,128)} copy(s32[2,8,8,128]{3,1,2,0:T(8,128)} %bitcast.8) | data formatting | bytes 131072
  2.1 7.4 %all-to-all-start = ((s32[16,8,128]{2,1,0:T(8,128)}), s32[16,8,128]{2,1,0:T(8,128)S(1)}, u32[]{:S(2)}, u32[]{:S(2)}) async-start(s32[16,8,128]{2,1,0:T(8,128)} %bitcast.6), calls=%async_computation | async-start | bytes 131072 | tf_op jit(solution)/shard_map/all_to_all | solution.py:512
  9.5 3.5 %shard_map.69.refs_1_ = f32[16,9,8,128]{3,2,1,0:T(8,128)} custom-call(f32[14,16384]{1,0:T(8,128)} %params_ref.3), custom_call_target="tpu_custom_call" | custom-call | tf_op jit(solution)/shard_map/pallas_call | solution.py:515
  13.0 3.4 %all-to-all-done.refs_0_.index_ref = s32[16,8,128]{2,1,0:T(8,128)S(1)} async-done(((s32[16,8,128]{2,1,0:T(8,128)}), s32[16,8,128]{2,1,0:T(8,128)S(1)}, u32[]{:S(2)}, u32[]{:S(2)}) %all-to-all-start) | async-done | bytes 65568 | tf_op jit(solution)/shard_map/all_to_all | solution.py:512
  16.4 0.6 copy-done.2
  17.0 13.1 %shard_map.70 = f32[16,9,8,128]{3,2,1,0:T(8,128)} custom-call(s32[16,8,128]{2,1,0:T(8,128)} %copy-done.2, f32[16,9,8,128]{3,2,1,0:T(8,128)} %shard_map.69.refs_1_), custom_call_target="tpu_custom_call" | custom-call | tf_op jit(solution)/shard_map/pallas_call | solution.py:505
  30.1 3.7 %all-to-all-start.1 = ((f32[16,9,8,128]{3,2,1,0:T(8,128)}), f32[16,9,8,128]{3,2,1,0:T(8,128)S(1)}, u32[]{:S(2)}, u32[]{:S(2)}) async-start(f32[16,9,8,128]{3,2,1,0:T(8,128)} %shard_map.70), calls=%async_computation.1 | async-start | bytes 1179648 | tf_op jit(solution)/shard_map/all_to_all | solution.py:492
  33.8 0.0 copy-start.3
  33.8 0.0 copy-done.5
  33.8 0.7 copy.13.upstream_ref
  34.5 0.1 copy-done.3
  34.7 0.2 reshape.17
  34.9 0.4 copy.10
  35.2 0.8 copy.12.index_ref.order_ref
  36.1 6.5 %shard_map.68.back_ref = s32[16,8,128]{2,1,0:T(8,128)} custom-call(s32[16,8,128]{2,1,0:T(8,128)} %copy.12.index_ref.order_ref), custom_call_target="tpu_custom_call" | custom-call | tf_op jit(solution)/shard_map/pallas_call | solution.py:498
  42.6 6.7 %all-to-all-done.1.arrived_ref = f32[16,9,8,128]{3,2,1,0:T(8,128)S(1)} async-done(((f32[16,9,8,128]{3,2,1,0:T(8,128)}), f32[16,9,8,128]{3,2,1,0:T(8,128)S(1)}, u32[]{:S(2)}, u32[]{:S(2)}) %all-to-all-start.1) | async-done | bytes 589856 | tf_op jit(solution)/shard_map/all_to_all | solution.py:492
  49.3 0.8 copy-done
  50.1 43.5 %shard_map.71 = (f32[16,3,256]{2,1,0:T(4,128)}, f32[16,9,8,128]{3,2,1,0:T(8,128)}) custom-call(s32[16]{0:T(128)} %count_ref.1, s32[1]{0:T(128)} %bitcast.first_ref, s32[16,8,128]{2,1,0:T(8,128)} %copy.12.index_ref.order_ref, s32[16,8,128]{2,1,0:T(8,128)} %shard_map.68.back_ref, f32[16,9,8,128]{3,2,1,0:T(8,128)} %copy-done, f32[16,3,256]{2,1,0:T(4,128)} %copy.13.upstream_ref), custom_call_target="tpu_custom_call" | custom-call | tf_op jit(solution)/shard_map/pallas_call | solution.py:533
  93.6 4.5 %all-to-all-start.2 = ((f32[16,9,8,128]{3,2,1,0:T(8,128)}), f32[16,9,8,128]{3,2,1,0:T(8,128)S(1)}, u32[]{:S(2)}, u32[]{:S(2)}) async-start(f32[16,9,8,128]{3,2,1,0:T(8,128)} %get-tuple-element.5), calls=%async_computation.2 | async-start | bytes 1179648 | tf_op jit(solution)/shard_map/all_to_all | solution.py:492
  98.1 6.6 %shard_map.72.index_ref = s32[16,8,128]{2,1,0:T(8,128)} custom-call(s32[16,8,128]{2,1,0:T(8,128)} %copy-done.2), custom_call_target="tpu_custom_call" | custom-call | tf_op jit(solution)/shard_map/pallas_call | solution.py:498
  104.7 0.6 copy.14
  105.3 8.3 %all-to-all-done.2.grads_ref = f32[16,9,8,128]{3,2,1,0:T(8,128)S(1)} async-done(((f32[16,9,8,128]{3,2,1,0:T(8,128)}), f32[16,9,8,128]{3,2,1,0:T(8,128)S(1)}, u32[]{:S(2)}, u32[]{:S(2)}) %all-to-all-start.2) | async-done | bytes 589856 | tf_op jit(solution)/shard_map/all_to_all | solution.py:492
  113.6 0.8 copy-done.1
  114.4 14.9 %shard_map.73 = f32[14,16384]{1,0:T(8,128)} custom-call(s32[16,8,128]{2,1,0:T(8,128)} %shard_map.72.index_ref, f32[16,9,8,128]{3,2,1,0:T(8,128)} %copy-done.1, f32[14,16384]{1,0:T(8,128)} %params_ref.3), custom_call_target="tpu_custom_call" | custom-call | tf_op jit(solution)/shard_map/pallas_call | solution.py:566
  (6 shorter events, 0.0 us)
Async XLA Ops:
  2.1 14.3 %all-to-all-start = ((s32[16,8,128]{2,1,0:T(8,128)}), s32[16,8,128]{2,1,0:T(8,128)S(1)}, u32[]{:S(2)}, u32[]{:S(2)}) async-start(s32[16,8,128]{2,1,0:T(8,128)} %bitcast.6), calls=%async_computation | async-start | bytes 131072 | tf_op jit(solution)/shard_map/all_to_all | solution.py:512
  16.4 0.6 copy-start.2
  30.1 3.7 %copy-start.5 = (f32[16,3,256]{2,0,1:T(8,128)S(1)}, f32[16,3,256]{2,0,1:T(8,128)}, u32[]{:S(2)}) copy-start(f32[16,3,256]{2,0,1:T(8,128)} %param.9) | copy-start | bytes 147460
  30.1 19.2 %all-to-all-start.1 = ((f32[16,9,8,128]{3,2,1,0:T(8,128)}), f32[16,9,8,128]{3,2,1,0:T(8,128)S(1)}, u32[]{:S(2)}, u32[]{:S(2)}) async-start(f32[16,9,8,128]{3,2,1,0:T(8,128)} %shard_map.70), calls=%async_computation.1 | async-start | bytes 1179648 | tf_op jit(solution)/shard_map/all_to_all | solution.py:492
  33.8 0.8 copy-start.3
  49.3 0.8 copy-start
  93.6 20.0 %all-to-all-start.2 = ((f32[16,9,8,128]{3,2,1,0:T(8,128)}), f32[16,9,8,128]{3,2,1,0:T(8,128)S(1)}, u32[]{:S(2)}, u32[]{:S(2)}) async-start(f32[16,9,8,128]{3,2,1,0:T(8,128)} %get-tuple-element.5), calls=%async_computation.2 | async-start | bytes 1179648 | tf_op jit(solution)/shard_map/all_to_all | solution.py:492
  98.1 6.6 %copy-start.4 = (f32[16,3,256]{2,1,0:T(4,128)S(1)}, f32[16,3,256]{2,1,0:T(4,128)}, u32[]{:S(2)}) copy-start(f32[16,3,256]{2,1,0:T(4,128)} %get-tuple-element.8) | copy-start | bytes 147460
  113.6 0.8 copy-start.1

commit v4 on v3

--- a/solution.py
+++ b/solution.py
@@ -12,6 +12,7 @@
 CHAN = 9
 PARAMS = 14
 LANED = 3
+AT_ONCE = 4
 FINE = 2
 WIDE = 8
 
@@ -69,15 +70,15 @@
     return out
 
 
-def gather_all(index_ref, in_ref, out_ref, table, table_low, fine):
+def gather_all(index_ref, in_ref, out_ref, table, table_low, fine, beside=None):
     groups = in_ref.shape[0]
+    quarter = groups // (ROWS // 2)
     fill_table(lambda c, half: read_half(in_ref, c, half), table, table_low, fine)
 
-    def step(t, carry):
+    def one(t):
         whole = index_ref[t]
         row, column = whole >> 7, whole & 127
         found = [jnp.zeros((ROWS, LANES), f32) for _ in range(LANED)]
-        quarter = groups // (ROWS // 2)
         for half in range(ROWS // 2):
             for q in range(half * quarter, half * quarter + quarter):
                 for s in range(ROWS):
@@ -96,9 +97,22 @@
                 out_ref[t, LANED + c, 2 * half + 1 : 2 * half + 2, :] = line[:, LANES:]
         for c in range(LANED):
             out_ref[t, c] = found[c]
+
+    def step(k, carry):
+        for u in range(AT_ONCE):
+            if beside is not None:
+                beside(jnp.maximum(k - 1, 0) * AT_ONCE + u)
+        for u in range(AT_ONCE):
+            one(k * AT_ONCE + u)
         return carry
 
-    lax.fori_loop(0, index_ref.shape[0], step, 0)
+    if beside is not None:
+        for u in range(AT_ONCE):
+            out_ref[u] = jnp.zeros_like(out_ref[u])
+    lax.fori_loop(0, groups // AT_ONCE, step, 0)
+    if beside is not None:
+        for u in range(AT_ONCE):
+            beside(groups - AT_ONCE + u)
 
 
 def invert_kernel(index_ref, out_ref):
@@ -212,9 +226,7 @@
 
 
 def return_kernel(index_ref, grads_ref, params_ref, out_ref, table, table_low, summed, raw, stage):
-    gather_all(index_ref, grads_ref, summed, table, table_low, 0)
-
-    def step(t, carry):
+    def back(t):
         for s in range(ROWS):
             raw[:, s, :] = params_ref[:, pl.ds(pl.multiple_of((t * ROWS + s) * LANES, LANES), LANES)]
         _, pull = jax.vjp(project_core, [raw[k] for k in range(10)])
@@ -226,9 +238,8 @@
             stage[11 + c] = summed[t, 6 + c]
         for s in range(ROWS):
             out_ref[:, pl.ds(pl.multiple_of((t * ROWS + s) * LANES, LANES), LANES)] = stage[:, s, :]
-        return carry
-
-    lax.fori_loop(0, grads_ref.shape[0], step, 0)
+
+    gather_all(index_ref, grads_ref, summed, table, table_low, 0, back)
 
 
 def scan_before(value, row):
@@ -347,7 +358,7 @@
             total = total + (b < count_ref[t]).astype(jnp.int32)
         return total
 
-    total = lax.fori_loop(0, tiles, prepare, jnp.int32(0))
+    total = lax.fori_loop(0, tiles, prepare, jnp.int32(0), unroll=2)
     for k in range(WIDE):
         live[total + k] = spare
     rounds = (total + WIDE - 1) // WIDE
@@ -399,7 +410,7 @@
             offset_s[t * blocks + b] = behind
         return carry
 
-    lax.fori_loop(0, tiles, scan_pass, 0)
+    lax.fori_loop(0, tiles, scan_pass, 0, unroll=2)
 
     def grad_pass(k, carry):
         for w in range(WIDE):
@@ -463,7 +474,7 @@
             grads_ref[t, 6 + c] = jnp.where(alive, colour_grads[t, c], 0.0)
         return carry
 
-    lax.fori_loop(0, tiles, finish, 0)
+    lax.fori_loop(0, tiles, finish, 0, unroll=2)
     gather_all(back_ref, grads_ref, sent_ref, table, table_low, 0)
 
 

time: 130 us -> 121 us (0.931)
  Pallas kernels: 88 us -> 79.5 us
    pallas_call x1, Pallas kernels: 43.5 us -> 39.9 us  [local(): pl.pallas_call(blend_kernel, in_specs=[pl.BlockSpec(memory_space=pltpu.SM...]
    pallas_call x1, Pallas kernels: 14.9 us -> 12.3 us  [local(): pl.pallas_call(return_kernel, out_shape=jax.ShapeDtypeStruct(gauss_params...]
    pallas_call x1, Pallas kernels: 13.1 us -> 10.7 us  [gather(): pl.pallas_call(lambda *refs: gather_kernel(fine, *refs), out_shape=jax.Sh...]
  transfers between devices with their start and end apart: 3 -> 3, of which waited for: 3 -> 3; matrix products, arithmetic and copies ran while one was open for 2% -> 2% of each run, Pallas kernels for 13% -> 14%
where the time goes in v4:
time: 121 us; the launch traced here: 120 us
  Pallas kernels  79.5 us (66%)
  waiting for transfers between devices  18.5 us (15%)
  starting transfers between devices  15 us (12%)
  local copies, waits for them, and re-layouts  6.59 us (5%)
    pallas_call x1, Pallas kernels, local(): pl.pallas_call(blend_kernel, in_specs=[pl.BlockSpec(memory_space=pltpu.SM...  39.9 us
    all_to_all x2, waiting for transfers between devices, exchange(): lax.all_to_all(value, 'tile', split_axis=0, concat_axis=0, tiled=True)  15.1 us
    pallas_call x2, Pallas kernels, invert(): pl.pallas_call(invert_kernel, out_shape=jax.ShapeDtypeStruct(index_shape,...  13.1 us
    pallas_call x1, Pallas kernels, local(): pl.pallas_call(return_kernel, out_shape=jax.ShapeDtypeStruct(gauss_params...  12.3 us
    pallas_call x1, Pallas kernels, gather(): pl.pallas_call(lambda *refs: gather_kernel(fine, *refs), out_shape=jax.Sh...  10.7 us
    all_to_all x2, starting transfers between devices, exchange(): lax.all_to_all(value, 'tile', split_axis=0, concat_axis=0, tiled=True)  7.64 us
    all_to_all x1, starting transfers between devices, local(): lax.all_to_all(wanted.reshape(peers, lines, LANES), 'tile', split_axis=0,...  7.39 us
    unnamed x15, local copies, waits for them, and re-layouts  5.21 us
  transfers between devices with their start and end apart: 3, of which 3 were waited for; matrix products, arithmetic and copies ran while one was open for 2% of the time, Pallas kernels for 14%

profile of v4, /device:TPU:0, one launch (start us, length us, event | category | flops | bytes accessed | tf_op | source)
XLA Modules:
  0.0 120.3 jit_solution(8598690047796843533)
XLA Ops:
  0.6 1.5 %copy.15 = s32[2,8,8,128]{3,2,1,0:T(8,128)} copy(s32[2,8,8,128]{3,1,2,0:T(8,128)} %bitcast.8) | data formatting | bytes 131072
  2.1 7.4 %all-to-all-start = ((s32[16,8,128]{2,1,0:T(8,128)}), s32[16,8,128]{2,1,0:T(8,128)S(1)}, u32[]{:S(2)}, u32[]{:S(2)}) async-start(s32[16,8,128]{2,1,0:T(8,128)} %bitcast.6), calls=%async_computation | async-start | bytes 131072 | tf_op jit(solution)/shard_map/all_to_all | solution.py:523
  9.5 3.5 %shard_map.69.refs_1_ = f32[16,9,8,128]{3,2,1,0:T(8,128)} custom-call(f32[14,16384]{1,0:T(8,128)} %params_ref.3), custom_call_target="tpu_custom_call" | custom-call | tf_op jit(solution)/shard_map/pallas_call | solution.py:526
  13.0 3.4 %all-to-all-done.refs_0_.index_ref = s32[16,8,128]{2,1,0:T(8,128)S(1)} async-done(((s32[16,8,128]{2,1,0:T(8,128)}), s32[16,8,128]{2,1,0:T(8,128)S(1)}, u32[]{:S(2)}, u32[]{:S(2)}) %all-to-all-start) | async-done | bytes 65568 | tf_op jit(solution)/shard_map/all_to_all | solution.py:523
  16.4 0.6 copy-done.2
  17.0 10.7 %shard_map.70 = f32[16,9,8,128]{3,2,1,0:T(8,128)} custom-call(s32[16,8,128]{2,1,0:T(8,128)} %copy-done.2, f32[16,9,8,128]{3,2,1,0:T(8,128)} %shard_map.69.refs_1_), custom_call_target="tpu_custom_call" | custom-call | tf_op jit(solution)/shard_map/pallas_call | solution.py:516
  27.8 3.7 %all-to-all-start.1 = ((f32[16,9,8,128]{3,2,1,0:T(8,128)}), f32[16,9,8,128]{3,2,1,0:T(8,128)S(1)}, u32[]{:S(2)}, u32[]{:S(2)}) async-start(f32[16,9,8,128]{3,2,1,0:T(8,128)} %shard_map.70), calls=%async_computation.1 | async-start | bytes 1179648 | tf_op jit(solution)/shard_map/all_to_all | solution.py:503
  31.5 0.0 copy-start.3
  31.5 0.7 copy.13.upstream_ref
  32.2 0.1 copy-done.3
  32.3 0.2 reshape.17
  32.5 0.4 copy.10
  32.9 0.8 copy.12.index_ref.order_ref
  33.7 6.5 %shard_map.68.back_ref = s32[16,8,128]{2,1,0:T(8,128)} custom-call(s32[16,8,128]{2,1,0:T(8,128)} %copy.12.index_ref.order_ref), custom_call_target="tpu_custom_call" | custom-call | tf_op jit(solution)/shard_map/pallas_call | solution.py:509
  40.3 6.7 %all-to-all-done.1.arrived_ref = f32[16,9,8,128]{3,2,1,0:T(8,128)S(1)} async-done(((f32[16,9,8,128]{3,2,1,0:T(8,128)}), f32[16,9,8,128]{3,2,1,0:T(8,128)S(1)}, u32[]{:S(2)}, u32[]{:S(2)}) %all-to-all-start.1) | async-done | bytes 589856 | tf_op jit(solution)/shard_map/all_to_all | solution.py:503
  47.0 0.8 copy-done
  47.8 39.9 %shard_map.71 = (f32[16,3,256]{2,1,0:T(4,128)}, f32[16,9,8,128]{3,2,1,0:T(8,128)}) custom-call(s32[16]{0:T(128)} %count_ref.1, s32[1]{0:T(128)} %bitcast.first_ref, s32[16,8,128]{2,1,0:T(8,128)} %copy.12.index_ref.order_ref, s32[16,8,128]{2,1,0:T(8,128)} %shard_map.68.back_ref, f32[16,9,8,128]{3,2,1,0:T(8,128)} %copy-done, f32[16,3,256]{2,1,0:T(4,128)} %copy.13.upstream_ref), custom_call_target="tpu_custom_call" | custom-call | tf_op jit(solution)/shard_map/pallas_call | solution.py:544
  87.7 3.9 %all-to-all-start.2 = ((f32[16,9,8,128]{3,2,1,0:T(8,128)}), f32[16,9,8,128]{3,2,1,0:T(8,128)S(1)}, u32[]{:S(2)}, u32[]{:S(2)}) async-start(f32[16,9,8,128]{3,2,1,0:T(8,128)} %get-tuple-element.5), calls=%async_computation.2 | async-start | bytes 1179648 | tf_op jit(solution)/shard_map/all_to_all | solution.py:503
  91.6 0.0 copy-start.4
  91.6 6.6 %shard_map.72.index_ref = s32[16,8,128]{2,1,0:T(8,128)} custom-call(s32[16,8,128]{2,1,0:T(8,128)} %copy-done.2), custom_call_target="tpu_custom_call" | custom-call | tf_op jit(solution)/shard_map/pallas_call | solution.py:509
  98.2 0.6 copy.14
  98.9 8.3 %all-to-all-done.2.grads_ref = f32[16,9,8,128]{3,2,1,0:T(8,128)S(1)} async-done(((f32[16,9,8,128]{3,2,1,0:T(8,128)}), f32[16,9,8,128]{3,2,1,0:T(8,128)S(1)}, u32[]{:S(2)}, u32[]{:S(2)}) %all-to-all-start.2) | async-done | bytes 589856 | tf_op jit(solution)/shard_map/all_to_all | solution.py:503
  107.2 0.8 copy-done.1
  108.0 12.3 %shard_map.73 = f32[14,16384]{1,0:T(8,128)} custom-call(s32[16,8,128]{2,1,0:T(8,128)} %shard_map.72.index_ref, f32[16,9,8,128]{3,2,1,0:T(8,128)} %copy-done.1, f32[14,16384]{1,0:T(8,128)} %params_ref.3), custom_call_target="tpu_custom_call" | custom-call | tf_op jit(solution)/shard_map/pallas_call | solution.py:577
  (6 shorter events, 0.0 us)
Async XLA Ops:
  2.1 14.3 %all-to-all-start = ((s32[16,8,128]{2,1,0:T(8,128)}), s32[16,8,128]{2,1,0:T(8,128)S(1)}, u32[]{:S(2)}, u32[]{:S(2)}) async-start(s32[16,8,128]{2,1,0:T(8,128)} %bitcast.6), calls=%async_computation | async-start | bytes 131072 | tf_op jit(solution)/shard_map/all_to_all | solution.py:523
  16.4 0.6 copy-start.2
  27.8 3.7 %copy-start.5 = (f32[16,3,256]{2,0,1:T(8,128)S(1)}, f32[16,3,256]{2,0,1:T(8,128)}, u32[]{:S(2)}) copy-start(f32[16,3,256]{2,0,1:T(8,128)} %param.9) | copy-start | bytes 147460
  27.8 19.2 %all-to-all-start.1 = ((f32[16,9,8,128]{3,2,1,0:T(8,128)}), f32[16,9,8,128]{3,2,1,0:T(8,128)S(1)}, u32[]{:S(2)}, u32[]{:S(2)}) async-start(f32[16,9,8,128]{3,2,1,0:T(8,128)} %shard_map.70), calls=%async_computation.1 | async-start | bytes 1179648 | tf_op jit(solution)/shard_map/all_to_all | solution.py:503
  31.5 0.8 copy-start.3
  47.0 0.8 copy-start
  87.7 19.5 %all-to-all-start.2 = ((f32[16,9,8,128]{3,2,1,0:T(8,128)}), f32[16,9,8,128]{3,2,1,0:T(8,128)S(1)}, u32[]{:S(2)}, u32[]{:S(2)}) async-start(f32[16,9,8,128]{3,2,1,0:T(8,128)} %get-tuple-element.5), calls=%async_computation.2 | async-start | bytes 1179648 | tf_op jit(solution)/shard_map/all_to_all | solution.py:503
  91.6 6.6 %copy-start.4 = (f32[16,3,256]{2,1,0:T(4,128)S(1)}, f32[16,3,256]{2,1,0:T(4,128)}, u32[]{:S(2)}) copy-start(f32[16,3,256]{2,1,0:T(4,128)} %get-tuple-element.8) | copy-start | bytes 147460
  107.2 0.8 copy-start.1

commit v5 on v4

--- a/solution.py
+++ b/solution.py
@@ -12,9 +12,11 @@
 CHAN = 9
 PARAMS = 14
 LANED = 3
-AT_ONCE = 4
+AT_ONCE = 8
+AT_ONCE_BACK = 4
 FINE = 2
-WIDE = 8
+LOCAL_WIDE = 16
+GRAD_WIDE = 8
 
 focal = 1000.0
 center_u = 512.0
@@ -70,7 +72,7 @@
     return out
 
 
-def gather_all(index_ref, in_ref, out_ref, table, table_low, fine, beside=None):
+def gather_all(index_ref, in_ref, out_ref, table, table_low, fine, beside=None, at_once=AT_ONCE):
     groups = in_ref.shape[0]
     quarter = groups // (ROWS // 2)
     fill_table(lambda c, half: read_half(in_ref, c, half), table, table_low, fine)
@@ -99,20 +101,20 @@
             out_ref[t, c] = found[c]
 
     def step(k, carry):
-        for u in range(AT_ONCE):
+        for u in range(at_once):
             if beside is not None:
-                beside(jnp.maximum(k - 1, 0) * AT_ONCE + u)
-        for u in range(AT_ONCE):
-            one(k * AT_ONCE + u)
+                beside(jnp.maximum(k - 1, 0) * at_once + u)
+        for u in range(at_once):
+            one(k * at_once + u)
         return carry
 
     if beside is not None:
-        for u in range(AT_ONCE):
+        for u in range(at_once):
             out_ref[u] = jnp.zeros_like(out_ref[u])
-    lax.fori_loop(0, groups // AT_ONCE, step, 0)
+    lax.fori_loop(0, groups // at_once, step, 0)
     if beside is not None:
-        for u in range(AT_ONCE):
-            beside(groups - AT_ONCE + u)
+        for u in range(at_once):
+            beside(groups - at_once + u)
 
 
 def invert_kernel(index_ref, out_ref):
@@ -239,7 +241,7 @@
         for s in range(ROWS):
             out_ref[:, pl.ds(pl.multiple_of((t * ROWS + s) * LANES, LANES), LANES)] = stage[:, s, :]
 
-    gather_all(index_ref, grads_ref, summed, table, table_low, 0, back)
+    gather_all(index_ref, grads_ref, summed, table, table_low, 0, back, AT_ONCE_BACK)
 
 
 def scan_before(value, row):
@@ -358,14 +360,13 @@
             total = total + (b < count_ref[t]).astype(jnp.int32)
         return total
 
-    total = lax.fori_loop(0, tiles, prepare, jnp.int32(0), unroll=2)
-    for k in range(WIDE):
+    total = lax.fori_loop(0, tiles, prepare, jnp.int32(0), unroll=4)
+    for k in range(LOCAL_WIDE):
         live[total + k] = spare
-    rounds = (total + WIDE - 1) // WIDE
 
     def local_pass(k, carry):
-        for w in range(WIDE):
-            name = live[k * WIDE + w]
+        for w in range(LOCAL_WIDE):
+            name = live[k * LOCAL_WIDE + w]
             block = features[name].astype(bf16)
             power = lax.dot_general(
                 block, power_basis, (((0,), (0,)), ((), ())), preferred_element_type=f32
@@ -390,7 +391,7 @@
             offset_s[name] = ahead
         return carry
 
-    lax.fori_loop(0, rounds, local_pass, 0)
+    lax.fori_loop(0, (total + LOCAL_WIDE - 1) // LOCAL_WIDE, local_pass, 0)
 
     def scan_pass(t, carry):
         trans = jnp.ones((1, PIX), f32)
@@ -410,11 +411,11 @@
             offset_s[t * blocks + b] = behind
         return carry
 
-    lax.fori_loop(0, tiles, scan_pass, 0, unroll=2)
+    lax.fori_loop(0, tiles, scan_pass, 0, unroll=4)
 
     def grad_pass(k, carry):
-        for w in range(WIDE):
-            name = live[k * WIDE + w]
+        for w in range(GRAD_WIDE):
+            name = live[k * GRAD_WIDE + w]
             t, b = name // blocks, name % blocks
             prod = gain_s[name]
             weights = []
@@ -450,7 +451,7 @@
             moments[t, :, b, :] = got[:, :BLOCK] + got[:, BLOCK:]
         return carry
 
-    lax.fori_loop(0, rounds, grad_pass, 0)
+    lax.fori_loop(0, (total + GRAD_WIDE - 1) // GRAD_WIDE, grad_pass, 0)
 
     def finish(t, carry):
         image_ref[t] = image_s[t, 0:3] + image_s[t, 3:6]
@@ -474,7 +475,7 @@
             grads_ref[t, 6 + c] = jnp.where(alive, colour_grads[t, c], 0.0)
         return carry
 
-    lax.fori_loop(0, tiles, finish, 0, unroll=2)
+    lax.fori_loop(0, tiles, finish, 0, unroll=4)
     gather_all(back_ref, grads_ref, sent_ref, table, table_low, 0)
 
 
@@ -559,7 +560,7 @@
         + [
             pltpu.VMEM((tiles_here, CHAN, blocks, BLOCK), f32),
             pltpu.VMEM((tiles_here, CHAN, blocks, BLOCK), f32),
-            pltpu.SMEM((spare + WIDE,), jnp.int32),
+            pltpu.SMEM((spare + LOCAL_WIDE,), jnp.int32),
             pltpu.VMEM((spare + 1, 32, BLOCK), f32),
             pltpu.VMEM((tiles_here + 1, 32, PIX), f32),
             pltpu.VMEM((tiles_here + 1, ROWS, PIX), f32),

time: 121 us -> 118 us (0.975)
  Pallas kernels: 79.5 us -> 69.5 us
  starting transfers between devices: 15 us -> 22.9 us
    pallas_call x1, Pallas kernels: 39.9 us -> 30.3 us  [local(): pl.pallas_call(blend_kernel, in_specs=[pl.BlockSpec(memory_space=pltpu.SM...]
    all_to_all x2, starting transfers between devices: 7.64 us -> 15.5 us  [exchange(): lax.all_to_all(value, 'tile', split_axis=0, concat_axis=0, tiled=True)]
where the time goes in v5:
time: 118 us
  Pallas kernels  69.5 us (59%)
  starting transfers between devices  22.9 us (19%)
  waiting for transfers between devices  18.5 us (16%)
  local copies, waits for them, and re-layouts  6.59 us (6%)
    pallas_call x1, Pallas kernels, local(): pl.pallas_call(blend_kernel, in_specs=[pl.BlockSpec(memory_space=pltpu.SM...  30.3 us
    all_to_all x2, starting transfers between devices, exchange(): lax.all_to_all(value, 'tile', split_axis=0, concat_axis=0, tiled=True)  15.5 us
    all_to_all x2, waiting for transfers between devices, exchange(): lax.all_to_all(value, 'tile', split_axis=0, concat_axis=0, tiled=True)  15.1 us
    pallas_call x2, Pallas kernels, invert(): pl.pallas_call(invert_kernel, out_shape=jax.ShapeDtypeStruct(index_shape,...  13.1 us
    pallas_call x1, Pallas kernels, local(): pl.pallas_call(return_kernel, out_shape=jax.ShapeDtypeStruct(gauss_params...  12.3 us
    pallas_call x1, Pallas kernels, gather(): pl.pallas_call(lambda *refs: gather_kernel(fine, *refs), out_shape=jax.Sh...  10.3 us
    all_to_all x1, starting transfers between devices, local(): lax.all_to_all(wanted.reshape(peers, lines, LANES), 'tile', split_axis=0,...  7.39 us
    unnamed x15, local copies, waits for them, and re-layouts  5.21 us
  transfers between devices with their start and end apart: 3, of which 3 were waited for; matrix products, arithmetic and copies ran while one was open for 2% of the time, Pallas kernels for 14%

profile of v5, /device:TPU:0, one launch (start us, length us, event | category | flops | bytes accessed | tf_op | source)
XLA Modules:
  0.0 118.2 jit_solution(1436581235384327145)
XLA Ops:
  0.6 1.5 %copy.15 = s32[2,8,8,128]{3,2,1,0:T(8,128)} copy(s32[2,8,8,128]{3,1,2,0:T(8,128)} %bitcast.8) | data formatting | bytes 131072
  2.1 7.4 %all-to-all-start = ((s32[16,8,128]{2,1,0:T(8,128)}), s32[16,8,128]{2,1,0:T(8,128)S(1)}, u32[]{:S(2)}, u32[]{:S(2)}) async-start(s32[16,8,128]{2,1,0:T(8,128)} %bitcast.6), calls=%async_computation | async-start | bytes 131072 | tf_op jit(solution)/shard_map/all_to_all | solution.py:524
  9.5 3.5 %shard_map.69.refs_1_ = f32[16,9,8,128]{3,2,1,0:T(8,128)} custom-call(f32[14,16384]{1,0:T(8,128)} %params_ref.3), custom_call_target="tpu_custom_call" | custom-call | tf_op jit(solution)/shard_map/pallas_call | solution.py:527
  13.0 3.4 %all-to-all-done.refs_0_.index_ref = s32[16,8,128]{2,1,0:T(8,128)S(1)} async-done(((s32[16,8,128]{2,1,0:T(8,128)}), s32[16,8,128]{2,1,0:T(8,128)S(1)}, u32[]{:S(2)}, u32[]{:S(2)}) %all-to-all-start) | async-done | bytes 65568 | tf_op jit(solution)/shard_map/all_to_all | solution.py:524
  16.4 0.6 copy-done.2
  17.0 10.3 %shard_map.70 = f32[16,9,8,128]{3,2,1,0:T(8,128)} custom-call(s32[16,8,128]{2,1,0:T(8,128)} %copy-done.2, f32[16,9,8,128]{3,2,1,0:T(8,128)} %shard_map.69.refs_1_), custom_call_target="tpu_custom_call" | custom-call | tf_op jit(solution)/shard_map/pallas_call | solution.py:517
  27.3 3.7 %all-to-all-start.1 = ((f32[16,9,8,128]{3,2,1,0:T(8,128)}), f32[16,9,8,128]{3,2,1,0:T(8,128)S(1)}, u32[]{:S(2)}, u32[]{:S(2)}) async-start(f32[16,9,8,128]{3,2,1,0:T(8,128)} %shard_map.70), calls=%async_computation.1 | async-start | bytes 1179648 | tf_op jit(solution)/shard_map/all_to_all | solution.py:504
  31.1 0.0 copy-start.3
  31.1 0.0 copy-done.5
  31.1 0.7 copy.13.upstream_ref
  31.7 0.1 copy-done.3
  31.9 0.2 reshape.17
  32.1 0.4 copy.10
  32.5 0.8 copy.12.index_ref.order_ref
  33.3 6.5 %shard_map.68.back_ref = s32[16,8,128]{2,1,0:T(8,128)} custom-call(s32[16,8,128]{2,1,0:T(8,128)} %copy.12.index_ref.order_ref), custom_call_target="tpu_custom_call" | custom-call | tf_op jit(solution)/shard_map/pallas_call | solution.py:510
  39.8 6.7 %all-to-all-done.1.arrived_ref = f32[16,9,8,128]{3,2,1,0:T(8,128)S(1)} async-done(((f32[16,9,8,128]{3,2,1,0:T(8,128)}), f32[16,9,8,128]{3,2,1,0:T(8,128)S(1)}, u32[]{:S(2)}, u32[]{:S(2)}) %all-to-all-start.1) | async-done | bytes 589856 | tf_op jit(solution)/shard_map/all_to_all | solution.py:504
  46.6 0.8 copy-done
  47.4 30.3 %shard_map.71 = (f32[16,3,256]{2,1,0:T(4,128)}, f32[16,9,8,128]{3,2,1,0:T(8,128)}) custom-call(s32[16]{0:T(128)} %count_ref.1, s32[1]{0:T(128)} %bitcast.first_ref, s32[16,8,128]{2,1,0:T(8,128)} %copy.12.index_ref.order_ref, s32[16,8,128]{2,1,0:T(8,128)} %shard_map.68.back_ref, f32[16,9,8,128]{3,2,1,0:T(8,128)} %copy-done, f32[16,3,256]{2,1,0:T(4,128)} %copy.13.upstream_ref), custom_call_target="tpu_custom_call" | custom-call | tf_op jit(solution)/shard_map/pallas_call | solution.py:545
  77.7 11.8 %all-to-all-start.2 = ((f32[16,9,8,128]{3,2,1,0:T(8,128)}), f32[16,9,8,128]{3,2,1,0:T(8,128)S(1)}, u32[]{:S(2)}, u32[]{:S(2)}) async-start(f32[16,9,8,128]{3,2,1,0:T(8,128)} %get-tuple-element.5), calls=%async_computation.2 | async-start | bytes 1179648 | tf_op jit(solution)/shard_map/all_to_all | solution.py:504
  89.5 6.6 %shard_map.72.index_ref = s32[16,8,128]{2,1,0:T(8,128)} custom-call(s32[16,8,128]{2,1,0:T(8,128)} %copy-done.2), custom_call_target="tpu_custom_call" | custom-call | tf_op jit(solution)/shard_map/pallas_call | solution.py:510
  96.1 0.6 copy.14
  96.7 8.3 %all-to-all-done.2.grads_ref = f32[16,9,8,128]{3,2,1,0:T(8,128)S(1)} async-done(((f32[16,9,8,128]{3,2,1,0:T(8,128)}), f32[16,9,8,128]{3,2,1,0:T(8,128)S(1)}, u32[]{:S(2)}, u32[]{:S(2)}) %all-to-all-start.2) | async-done | bytes 589856 | tf_op jit(solution)/shard_map/all_to_all | solution.py:504
  105.1 0.8 copy-done.1
  105.9 12.3 %shard_map.73 = f32[14,16384]{1,0:T(8,128)} custom-call(s32[16,8,128]{2,1,0:T(8,128)} %shard_map.72.index_ref, f32[16,9,8,128]{3,2,1,0:T(8,128)} %copy-done.1, f32[14,16384]{1,0:T(8,128)} %params_ref.3), custom_call_target="tpu_custom_call" | custom-call | tf_op jit(solution)/shard_map/pallas_call | solution.py:578
  (6 shorter events, 0.0 us)
Async XLA Ops:
  2.1 14.3 %all-to-all-start = ((s32[16,8,128]{2,1,0:T(8,128)}), s32[16,8,128]{2,1,0:T(8,128)S(1)}, u32[]{:S(2)}, u32[]{:S(2)}) async-start(s32[16,8,128]{2,1,0:T(8,128)} %bitcast.6), calls=%async_computation | async-start | bytes 131072 | tf_op jit(solution)/shard_map/all_to_all | solution.py:524
  16.4 0.6 copy-start.2
  27.3 3.7 %copy-start.5 = (f32[16,3,256]{2,0,1:T(8,128)S(1)}, f32[16,3,256]{2,0,1:T(8,128)}, u32[]{:S(2)}) copy-start(f32[16,3,256]{2,0,1:T(8,128)} %param.9) | copy-start | bytes 147460
  27.3 19.2 %all-to-all-start.1 = ((f32[16,9,8,128]{3,2,1,0:T(8,128)}), f32[16,9,8,128]{3,2,1,0:T(8,128)S(1)}, u32[]{:S(2)}, u32[]{:S(2)}) async-start(f32[16,9,8,128]{3,2,1,0:T(8,128)} %shard_map.70), calls=%async_computation.1 | async-start | bytes 1179648 | tf_op jit(solution)/shard_map/all_to_all | solution.py:504
  31.1 0.8 copy-start.3
  46.6 0.8 copy-start
  77.7 27.4 %all-to-all-start.2 = ((f32[16,9,8,128]{3,2,1,0:T(8,128)}), f32[16,9,8,128]{3,2,1,0:T(8,128)S(1)}, u32[]{:S(2)}, u32[]{:S(2)}) async-start(f32[16,9,8,128]{3,2,1,0:T(8,128)} %get-tuple-element.5), calls=%async_computation.2 | async-start | bytes 1179648 | tf_op jit(solution)/shard_map/all_to_all | solution.py:504
  89.5 6.6 %copy-start.4 = (f32[16,3,256]{2,1,0:T(4,128)S(1)}, f32[16,3,256]{2,1,0:T(4,128)}, u32[]{:S(2)}) copy-start(f32[16,3,256]{2,1,0:T(4,128)} %get-tuple-element.8) | copy-start | bytes 147460
  105.1 0.8 copy-start.1

commit v6 on v5

--- a/solution.py
+++ b/solution.py
@@ -72,10 +72,11 @@
     return out
 
 
-def gather_all(index_ref, in_ref, out_ref, table, table_low, fine, beside=None, at_once=AT_ONCE):
+def gather_all(index_ref, in_ref, out_ref, table, table_low, fine, beside=None, at_once=AT_ONCE, filled=False):
     groups = in_ref.shape[0]
     quarter = groups // (ROWS // 2)
-    fill_table(lambda c, half: read_half(in_ref, c, half), table, table_low, fine)
+    if not filled:
+        fill_table(lambda c, half: read_half(in_ref, c, half), table, table_low, fine)
 
     def one(t):
         whole = index_ref[t]
@@ -203,7 +204,7 @@
     return 1.0 / (1.0 + jnp.exp(-x))
 
 
-def project_kernel(params_ref, out_ref, raw):
+def project_kernel(params_ref, out_ref, table, table_low, raw):
     def step(t, carry):
         for s in range(ROWS):
             raw[:, s, :] = params_ref[:, pl.ds(pl.multiple_of((t * ROWS + s) * LANES, LANES), LANES)]
@@ -216,6 +217,7 @@
         return carry
 
     lax.fori_loop(0, out_ref.shape[0], step, 0)
+    fill_table(lambda c, half: read_half(out_ref, c, half), table, table_low, FINE)
 
 
 def read_half(ref, c, half):
@@ -223,8 +225,8 @@
     return jnp.concatenate([ref[half * groups + q, c] for q in range(groups)], axis=0)
 
 
-def gather_kernel(fine, index_ref, in_ref, out_ref, table, table_low):
-    gather_all(index_ref, in_ref, out_ref, table, table_low, fine)
+def gather_kernel(index_ref, in_ref, table, table_low, out_ref):
+    gather_all(index_ref, in_ref, out_ref, table, table_low, FINE, filled=True)
 
 
 def return_kernel(index_ref, grads_ref, params_ref, out_ref, table, table_low, summed, raw, stage):
@@ -513,20 +515,16 @@
             compiler_params=params(),
         )(index)
 
-    def gather(index, value, fine):
-        return pl.pallas_call(
-            lambda *refs: gather_kernel(fine, *refs),
-            out_shape=jax.ShapeDtypeStruct(shape, f32),
-            scratch_shapes=tables,
-            compiler_params=params(),
-        )(index, value)
-
     asked = lax.all_to_all(
         wanted.reshape(peers, lines, LANES), "tile", split_axis=0, concat_axis=0, tiled=True
     ).reshape(index_shape)
     projected = pl.pallas_call(
         project_kernel,
-        out_shape=jax.ShapeDtypeStruct(shape, f32),
+        out_shape=[
+            jax.ShapeDtypeStruct(shape, f32),
+            jax.ShapeDtypeStruct(((CHAN - LANED) * 64, 512), bf16),
+            jax.ShapeDtypeStruct((FINE * 64, 256), bf16),
+        ],
         scratch_shapes=[pltpu.VMEM((PARAMS, ROWS, LANES), f32)],
         compiler_params=params(),
     )(gauss_params)
@@ -536,7 +534,11 @@
         .reshape(tiles_here, blocks, BLOCK)
     )
     order_back = invert(order)
-    outgoing = gather(asked, projected, FINE)
+    outgoing = pl.pallas_call(
+        gather_kernel,
+        out_shape=jax.ShapeDtypeStruct(shape, f32),
+        compiler_params=params(),
+    )(asked, *projected)
     arrived = exchange(outgoing)
     asked_back = invert(asked)
     first_tile = (lax.axis_index("tile") * tiles_here).reshape(1).astype(jnp.int32)

time: 118 us -> 118 us (level); the launches traced: 118 us -> 116 us
  starting transfers between devices: 22.9 us -> 16 us
  Pallas kernels: 69.5 us -> 74.9 us
    all_to_all x2, starting transfers between devices: 15.5 us -> 8.63 us  [exchange(): lax.all_to_all(value, 'tile', split_axis=0, concat_axis=0, tiled=True)]
    pallas_call x1, Pallas kernels: 30.3 us -> 35.5 us  [local(): pl.pallas_call(blend_kernel, in_specs=[pl.BlockSpec(memory_space=pltpu.SM...]
where the time goes in v6:
time: 118 us; the launch traced here: 116 us
  Pallas kernels  74.9 us (63%)
  waiting for transfers between devices  18.5 us (16%)
  starting transfers between devices  16 us (14%)
  local copies, waits for them, and re-layouts  6.38 us (5%)
    pallas_call x1, Pallas kernels, local(): pl.pallas_call(blend_kernel, in_specs=[pl.BlockSpec(memory_space=pltpu.SM...  35.5 us
    all_to_all x2, waiting for transfers between devices, exchange(): lax.all_to_all(value, 'tile', split_axis=0, concat_axis=0, tiled=True)  15.2 us
    pallas_call x2, Pallas kernels, invert(): pl.pallas_call(invert_kernel, out_shape=jax.ShapeDtypeStruct(index_shape,...  13.1 us
    pallas_call x1, Pallas kernels, local(): pl.pallas_call(return_kernel, out_shape=jax.ShapeDtypeStruct(gauss_params...  12.3 us
    pallas_call x1, Pallas kernels, local(): pl.pallas_call(gather_kernel, out_shape=jax.ShapeDtypeStruct(shape, f32),...  10.3 us
    all_to_all x2, starting transfers between devices, exchange(): lax.all_to_all(value, 'tile', split_axis=0, concat_axis=0, tiled=True)  8.63 us
    all_to_all x1, starting transfers between devices, local(): lax.all_to_all(wanted.reshape(peers, lines, LANES), 'tile', split_axis=0,...  7.39 us
    unnamed x15, local copies, waits for them, and re-layouts  5.01 us
  transfers between devices with their start and end apart: 3, of which 3 were waited for; matrix products, arithmetic and copies ran while one was open for 2% of the time, Pallas kernels for 14%

profile of v6, /device:TPU:0, one launch (start us, length us, event | category | flops | bytes accessed | tf_op | source)
XLA Modules:
  0.0 116.5 jit_solution(5404526739776461380)
XLA Ops:
  0.6 1.5 %copy.15 = s32[2,8,8,128]{3,2,1,0:T(8,128)} copy(s32[2,8,8,128]{3,1,2,0:T(8,128)} %bitcast.8) | data formatting | bytes 131072
  2.1 7.4 %all-to-all-start = ((s32[16,8,128]{2,1,0:T(8,128)}), s32[16,8,128]{2,1,0:T(8,128)S(1)}, u32[]{:S(2)}, u32[]{:S(2)}) async-start(s32[16,8,128]{2,1,0:T(8,128)} %bitcast.6), calls=%async_computation | async-start | bytes 131072 | tf_op jit(solution)/shard_map/all_to_all | solution.py:518
  9.5 3.6 %shard_map.69 = (f32[16,9,8,128]{3,2,1,0:T(8,128)}, bf16[384,512]{1,0:T(8,128)(2,1)}, bf16[128,256]{1,0:T(8,128)(2,1)}) custom-call(f32[14,16384]{1,0:T(8,128)} %params_ref.3), custom_call_target="tpu_custom_call" | custom-call | tf_op jit(solution)/shard_map/pallas_call | solution.py:521
  13.1 3.3 %all-to-all-done.index_ref = s32[16,8,128]{2,1,0:T(8,128)S(1)} async-done(((s32[16,8,128]{2,1,0:T(8,128)}), s32[16,8,128]{2,1,0:T(8,128)S(1)}, u32[]{:S(2)}, u32[]{:S(2)}) %all-to-all-start) | async-done | bytes 65568 | tf_op jit(solution)/shard_map/all_to_all | solution.py:518
  16.4 0.6 copy-done.2
  17.0 10.3 %shard_map.70 = f32[16,9,8,128]{3,2,1,0:T(8,128)} custom-call(s32[16,8,128]{2,1,0:T(8,128)} %copy-done.2, f32[16,9,8,128]{3,2,1,0:T(8,128)} %get-tuple-element.7.in_ref, bf16[384,512]{1,0:T(8,128)(2,1)} %get-tuple-element.8.table, bf16[128,256]{1,0:T(8,128)(2,1)} %get-tuple-element.9.table_low), custom_call_target="tpu_custom_call" | custom-call | tf_op jit(solution)/shard_map/pallas_call | solution.py:537
  27.3 3.7 %all-to-all-start.1 = ((f32[16,9,8,128]{3,2,1,0:T(8,128)}), f32[16,9,8,128]{3,2,1,0:T(8,128)S(1)}, u32[]{:S(2)}, u32[]{:S(2)}) async-start(f32[16,9,8,128]{3,2,1,0:T(8,128)} %shard_map.70), calls=%async_computation.1 | async-start | bytes 1179648 | tf_op jit(solution)/shard_map/all_to_all | solution.py:506
  31.1 0.0 copy-done.3
  31.1 0.2 reshape.17
  31.3 0.4 copy.10
  31.7 0.8 copy.12.index_ref.order_ref
  32.5 6.6 %shard_map.68.back_ref = s32[16,8,128]{2,1,0:T(8,128)} custom-call(s32[16,8,128]{2,1,0:T(8,128)} %copy.12.index_ref.order_ref), custom_call_target="tpu_custom_call" | custom-call | tf_op jit(solution)/shard_map/pallas_call | solution.py:512
  39.0 0.0 copy-done.5
  39.0 0.6 copy.13.upstream_ref
  39.7 6.9 %all-to-all-done.1.arrived_ref = f32[16,9,8,128]{3,2,1,0:T(8,128)S(1)} async-done(((f32[16,9,8,128]{3,2,1,0:T(8,128)}), f32[16,9,8,128]{3,2,1,0:T(8,128)S(1)}, u32[]{:S(2)}, u32[]{:S(2)}) %all-to-all-start.1) | async-done | bytes 589856 | tf_op jit(solution)/shard_map/all_to_all | solution.py:506
  46.6 0.8 copy-done
  47.4 35.5 %shard_map.71 = (f32[16,3,256]{2,1,0:T(4,128)}, f32[16,9,8,128]{3,2,1,0:T(8,128)}) custom-call(s32[16]{0:T(128)} %count_ref.1, s32[1]{0:T(128)} %bitcast.first_ref, s32[16,8,128]{2,1,0:T(8,128)} %copy.12.index_ref.order_ref, s32[16,8,128]{2,1,0:T(8,128)} %shard_map.68.back_ref, f32[16,9,8,128]{3,2,1,0:T(8,128)} %copy-done, f32[16,3,256]{2,1,0:T(4,128)} %copy.13.upstream_ref), custom_call_target="tpu_custom_call" | custom-call | tf_op jit(solution)/shard_map/pallas_call | solution.py:547
  82.9 4.9 %all-to-all-start.2 = ((f32[16,9,8,128]{3,2,1,0:T(8,128)}), f32[16,9,8,128]{3,2,1,0:T(8,128)S(1)}, u32[]{:S(2)}, u32[]{:S(2)}) async-start(f32[16,9,8,128]{3,2,1,0:T(8,128)} %get-tuple-element.11), calls=%async_computation.2 | async-start | bytes 1179648 | tf_op jit(solution)/shard_map/all_to_all | solution.py:506
  87.8 0.0 copy-start.4
  87.8 6.6 %shard_map.72.index_ref = s32[16,8,128]{2,1,0:T(8,128)} custom-call(s32[16,8,128]{2,1,0:T(8,128)} %copy-done.2), custom_call_target="tpu_custom_call" | custom-call | tf_op jit(solution)/shard_map/pallas_call | solution.py:512
  94.4 0.6 copy.14
  95.0 8.3 %all-to-all-done.2.grads_ref = f32[16,9,8,128]{3,2,1,0:T(8,128)S(1)} async-done(((f32[16,9,8,128]{3,2,1,0:T(8,128)}), f32[16,9,8,128]{3,2,1,0:T(8,128)S(1)}, u32[]{:S(2)}, u32[]{:S(2)}) %all-to-all-start.2) | async-done | bytes 589856 | tf_op jit(solution)/shard_map/all_to_all | solution.py:506
  103.4 0.8 copy-done.1
  104.2 12.3 %shard_map.73 = f32[14,16384]{1,0:T(8,128)} custom-call(s32[16,8,128]{2,1,0:T(8,128)} %shard_map.72.index_ref, f32[16,9,8,128]{3,2,1,0:T(8,128)} %copy-done.1, f32[14,16384]{1,0:T(8,128)} %params_ref.3), custom_call_target="tpu_custom_call" | custom-call | tf_op jit(solution)/shard_map/pallas_call | solution.py:580
  (6 shorter events, 0.0 us)
Async XLA Ops:
  2.1 14.3 %all-to-all-start = ((s32[16,8,128]{2,1,0:T(8,128)}), s32[16,8,128]{2,1,0:T(8,128)S(1)}, u32[]{:S(2)}, u32[]{:S(2)}) async-start(s32[16,8,128]{2,1,0:T(8,128)} %bitcast.6), calls=%async_computation | async-start | bytes 131072 | tf_op jit(solution)/shard_map/all_to_all | solution.py:518
  16.4 0.6 copy-start.2
  27.3 3.7 %copy-start.3 = (s32[16,1024]{1,0:T(8,128)S(1)}, s32[16,1024]{1,0:T(8,128)}, u32[]{:S(2)}) copy-start(s32[16,1024]{1,0:T(8,128)} %param.7) | copy-start | bytes 196612
  27.3 19.2 %all-to-all-start.1 = ((f32[16,9,8,128]{3,2,1,0:T(8,128)}), f32[16,9,8,128]{3,2,1,0:T(8,128)S(1)}, u32[]{:S(2)}, u32[]{:S(2)}) async-start(f32[16,9,8,128]{3,2,1,0:T(8,128)} %shard_map.70), calls=%async_computation.1 | async-start | bytes 1179648 | tf_op jit(solution)/shard_map/all_to_all | solution.py:506
  32.4 6.6 %copy-start.5 = (f32[16,3,256]{2,0,1:T(8,128)S(1)}, f32[16,3,256]{2,0,1:T(8,128)}, u32[]{:S(2)}) copy-start(f32[16,3,256]{2,0,1:T(8,128)} %param.9) | copy-start | bytes 147460
  46.6 0.8 copy-start
  82.9 20.5 %all-to-all-start.2 = ((f32[16,9,8,128]{3,2,1,0:T(8,128)}), f32[16,9,8,128]{3,2,1,0:T(8,128)S(1)}, u32[]{:S(2)}, u32[]{:S(2)}) async-start(f32[16,9,8,128]{3,2,1,0:T(8,128)} %get-tuple-element.11), calls=%async_computation.2 | async-start | bytes 1179648 | tf_op jit(solution)/shard_map/all_to_all | solution.py:506
  87.8 6.6 %copy-start.4 = (f32[16,3,256]{2,1,0:T(4,128)S(1)}, f32[16,3,256]{2,1,0:T(4,128)}, u32[]{:S(2)}) copy-start(f32[16,3,256]{2,1,0:T(4,128)} %get-tuple-element.14) | copy-start | bytes 147460
  103.4 0.8 copy-start.1

commit v7 on v6

--- a/solution.py
+++ b/solution.py
@@ -270,8 +270,8 @@
 
 
 def split_stack(values):
-    both = [two_rows(value) for value in values]
-    return jnp.concatenate([head for head, _ in both] + [tail for _, tail in both], axis=0)
+    head, tail = two_rows(jnp.concatenate(values, axis=0))
+    return jnp.concatenate([head, tail], axis=0)
 
 
 def blend_kernel(

time: 118 us -> 117 us (level)
  Pallas kernels: 74.9 us -> 67.6 us
  starting transfers between devices: 16 us -> 23.3 us
    pallas_call x1, Pallas kernels: 35.5 us -> 28.2 us  [local(): pl.pallas_call(blend_kernel, in_specs=[pl.BlockSpec(memory_space=pltpu.SM...]
    all_to_all x2, starting transfers between devices: 8.63 us -> 15.9 us  [exchange(): lax.all_to_all(value, 'tile', split_axis=0, concat_axis=0, tiled=True)]
where the time goes in v7:
time: 117 us; the launch traced here: 116 us
  Pallas kernels  67.6 us (58%)
  starting transfers between devices  23.3 us (20%)
  waiting for transfers between devices  18.5 us (16%)
  local copies, waits for them, and re-layouts  6.38 us (5%)
    pallas_call x1, Pallas kernels, local(): pl.pallas_call(blend_kernel, in_specs=[pl.BlockSpec(memory_space=pltpu.SM...  28.2 us
    all_to_all x2, starting transfers between devices, exchange(): lax.all_to_all(value, 'tile', split_axis=0, concat_axis=0, tiled=True)  15.9 us
    all_to_all x2, waiting for transfers between devices, exchange(): lax.all_to_all(value, 'tile', split_axis=0, concat_axis=0, tiled=True)  15.2 us
    pallas_call x2, Pallas kernels, invert(): pl.pallas_call(invert_kernel, out_shape=jax.ShapeDtypeStruct(index_shape,...  13.1 us
    pallas_call x1, Pallas kernels, local(): pl.pallas_call(return_kernel, out_shape=jax.ShapeDtypeStruct(gauss_params...  12.3 us
    pallas_call x1, Pallas kernels, local(): pl.pallas_call(gather_kernel, out_shape=jax.ShapeDtypeStruct(shape, f32),...  10.3 us
    all_to_all x1, starting transfers between devices, local(): lax.all_to_all(wanted.reshape(peers, lines, LANES), 'tile', split_axis=0,...  7.39 us
    unnamed x15, local copies, waits for them, and re-layouts  5.01 us
  transfers between devices with their start and end apart: 3, of which 3 were waited for; matrix products, arithmetic and copies ran while one was open for 2% of the time, Pallas kernels for 14%

profile of v7, /device:TPU:0, one launch (start us, length us, event | category | flops | bytes accessed | tf_op | source)
XLA Modules:
  0.0 116.5 jit_solution(1197655817696080493)
XLA Ops:
  0.6 1.5 %copy.15 = s32[2,8,8,128]{3,2,1,0:T(8,128)} copy(s32[2,8,8,128]{3,1,2,0:T(8,128)} %bitcast.8) | data formatting | bytes 131072
  2.1 7.4 %all-to-all-start = ((s32[16,8,128]{2,1,0:T(8,128)}), s32[16,8,128]{2,1,0:T(8,128)S(1)}, u32[]{:S(2)}, u32[]{:S(2)}) async-start(s32[16,8,128]{2,1,0:T(8,128)} %bitcast.6), calls=%async_computation | async-start | bytes 131072 | tf_op jit(solution)/shard_map/all_to_all | solution.py:518
  9.5 3.6 %shard_map.69 = (f32[16,9,8,128]{3,2,1,0:T(8,128)}, bf16[384,512]{1,0:T(8,128)(2,1)}, bf16[128,256]{1,0:T(8,128)(2,1)}) custom-call(f32[14,16384]{1,0:T(8,128)} %params_ref.3), custom_call_target="tpu_custom_call" | custom-call | tf_op jit(solution)/shard_map/pallas_call | solution.py:521
  13.1 3.3 %all-to-all-done.index_ref = s32[16,8,128]{2,1,0:T(8,128)S(1)} async-done(((s32[16,8,128]{2,1,0:T(8,128)}), s32[16,8,128]{2,1,0:T(8,128)S(1)}, u32[]{:S(2)}, u32[]{:S(2)}) %all-to-all-start) | async-done | bytes 65568 | tf_op jit(solution)/shard_map/all_to_all | solution.py:518
  16.4 0.6 copy-done.2
  17.0 10.3 %shard_map.70 = f32[16,9,8,128]{3,2,1,0:T(8,128)} custom-call(s32[16,8,128]{2,1,0:T(8,128)} %copy-done.2, f32[16,9,8,128]{3,2,1,0:T(8,128)} %get-tuple-element.7.in_ref, bf16[384,512]{1,0:T(8,128)(2,1)} %get-tuple-element.8.table, bf16[128,256]{1,0:T(8,128)(2,1)} %get-tuple-element.9.table_low), custom_call_target="tpu_custom_call" | custom-call | tf_op jit(solution)/shard_map/pallas_call | solution.py:537
  27.3 3.7 %all-to-all-start.1 = ((f32[16,9,8,128]{3,2,1,0:T(8,128)}), f32[16,9,8,128]{3,2,1,0:T(8,128)S(1)}, u32[]{:S(2)}, u32[]{:S(2)}) async-start(f32[16,9,8,128]{3,2,1,0:T(8,128)} %shard_map.70), calls=%async_computation.1 | async-start | bytes 1179648 | tf_op jit(solution)/shard_map/all_to_all | solution.py:506
  31.1 0.0 copy-done.3
  31.1 0.2 reshape.17
  31.3 0.4 copy.10
  31.7 0.8 copy.12.index_ref.order_ref
  32.5 6.6 %shard_map.68.back_ref = s32[16,8,128]{2,1,0:T(8,128)} custom-call(s32[16,8,128]{2,1,0:T(8,128)} %copy.12.index_ref.order_ref), custom_call_target="tpu_custom_call" | custom-call | tf_op jit(solution)/shard_map/pallas_call | solution.py:512
  39.0 0.0 copy-done.5
  39.0 0.6 copy.13.upstream_ref
  39.7 6.9 %all-to-all-done.1.arrived_ref = f32[16,9,8,128]{3,2,1,0:T(8,128)S(1)} async-done(((f32[16,9,8,128]{3,2,1,0:T(8,128)}), f32[16,9,8,128]{3,2,1,0:T(8,128)S(1)}, u32[]{:S(2)}, u32[]{:S(2)}) %all-to-all-start.1) | async-done | bytes 589856 | tf_op jit(solution)/shard_map/all_to_all | solution.py:506
  46.6 0.8 copy-done
  47.4 28.2 %shard_map.71 = (f32[16,3,256]{2,1,0:T(4,128)}, f32[16,9,8,128]{3,2,1,0:T(8,128)}) custom-call(s32[16]{0:T(128)} %count_ref.1, s32[1]{0:T(128)} %bitcast.first_ref, s32[16,8,128]{2,1,0:T(8,128)} %copy.12.index_ref.order_ref, s32[16,8,128]{2,1,0:T(8,128)} %shard_map.68.back_ref, f32[16,9,8,128]{3,2,1,0:T(8,128)} %copy-done, f32[16,3,256]{2,1,0:T(4,128)} %copy.13.upstream_ref), custom_call_target="tpu_custom_call" | custom-call | tf_op jit(solution)/shard_map/pallas_call | solution.py:547
  75.6 12.2 %all-to-all-start.2 = ((f32[16,9,8,128]{3,2,1,0:T(8,128)}), f32[16,9,8,128]{3,2,1,0:T(8,128)S(1)}, u32[]{:S(2)}, u32[]{:S(2)}) async-start(f32[16,9,8,128]{3,2,1,0:T(8,128)} %get-tuple-element.11), calls=%async_computation.2 | async-start | bytes 1179648 | tf_op jit(solution)/shard_map/all_to_all | solution.py:506
  87.8 0.0 copy-start.4
  87.8 6.6 %shard_map.72.index_ref = s32[16,8,128]{2,1,0:T(8,128)} custom-call(s32[16,8,128]{2,1,0:T(8,128)} %copy-done.2), custom_call_target="tpu_custom_call" | custom-call | tf_op jit(solution)/shard_map/pallas_call | solution.py:512
  94.4 0.6 copy.14
  95.0 8.3 %all-to-all-done.2.grads_ref = f32[16,9,8,128]{3,2,1,0:T(8,128)S(1)} async-done(((f32[16,9,8,128]{3,2,1,0:T(8,128)}), f32[16,9,8,128]{3,2,1,0:T(8,128)S(1)}, u32[]{:S(2)}, u32[]{:S(2)}) %all-to-all-start.2) | async-done | bytes 589856 | tf_op jit(solution)/shard_map/all_to_all | solution.py:506
  103.4 0.8 copy-done.1
  104.2 12.3 %shard_map.73 = f32[14,16384]{1,0:T(8,128)} custom-call(s32[16,8,128]{2,1,0:T(8,128)} %shard_map.72.index_ref, f32[16,9,8,128]{3,2,1,0:T(8,128)} %copy-done.1, f32[14,16384]{1,0:T(8,128)} %params_ref.3), custom_call_target="tpu_custom_call" | custom-call | tf_op jit(solution)/shard_map/pallas_call | solution.py:580
  (6 shorter events, 0.0 us)
Async XLA Ops:
  2.1 14.3 %all-to-all-start = ((s32[16,8,128]{2,1,0:T(8,128)}), s32[16,8,128]{2,1,0:T(8,128)S(1)}, u32[]{:S(2)}, u32[]{:S(2)}) async-start(s32[16,8,128]{2,1,0:T(8,128)} %bitcast.6), calls=%async_computation | async-start | bytes 131072 | tf_op jit(solution)/shard_map/all_to_all | solution.py:518
  16.4 0.6 copy-start.2
  27.3 3.7 %copy-start.3 = (s32[16,1024]{1,0:T(8,128)S(1)}, s32[16,1024]{1,0:T(8,128)}, u32[]{:S(2)}) copy-start(s32[16,1024]{1,0:T(8,128)} %param.7) | copy-start | bytes 196612
  27.3 19.2 %all-to-all-start.1 = ((f32[16,9,8,128]{3,2,1,0:T(8,128)}), f32[16,9,8,128]{3,2,1,0:T(8,128)S(1)}, u32[]{:S(2)}, u32[]{:S(2)}) async-start(f32[16,9,8,128]{3,2,1,0:T(8,128)} %shard_map.70), calls=%async_computation.1 | async-start | bytes 1179648 | tf_op jit(solution)/shard_map/all_to_all | solution.py:506
  32.4 6.6 %copy-start.5 = (f32[16,3,256]{2,0,1:T(8,128)S(1)}, f32[16,3,256]{2,0,1:T(8,128)}, u32[]{:S(2)}) copy-start(f32[16,3,256]{2,0,1:T(8,128)} %param.9) | copy-start | bytes 147460
  46.6 0.8 copy-start
  75.6 27.8 %all-to-all-start.2 = ((f32[16,9,8,128]{3,2,1,0:T(8,128)}), f32[16,9,8,128]{3,2,1,0:T(8,128)S(1)}, u32[]{:S(2)}, u32[]{:S(2)}) async-start(f32[16,9,8,128]{3,2,1,0:T(8,128)} %get-tuple-element.11), calls=%async_computation.2 | async-start | bytes 1179648 | tf_op jit(solution)/shard_map/all_to_all | solution.py:506
  87.8 6.6 %copy-start.4 = (f32[16,3,256]{2,1,0:T(4,128)S(1)}, f32[16,3,256]{2,1,0:T(4,128)}, u32[]{:S(2)}) copy-start(f32[16,3,256]{2,1,0:T(4,128)} %get-tuple-element.14) | copy-start | bytes 147460
  103.4 0.8 copy-start.1
